TPU v7x, 32 devices: a whole 2x2x4 slice. The times are simulated.
32 devices in a mesh: row: 16 (over z, y, core), rep: 2 (over x).
Axes of the slice: x: 2, y: 2, z: 4, core: 2. Of those that a mesh axis runs over, the one named last changes fastest.
Arguments:
- features: bfloat16 [12288, 256], P('row'), may hold values from -7 to 7
- adjacency: bfloat16 [12288, 12288], P('row', 'rep'), may hold values from -0.078125 to 0.078125
- tile_live: int32 [16, 16], P('row', 'rep'), may hold values from 0 to 1, as said below
- w_self: bfloat16 [256, 256], replicated, may hold values from -1.25 to 1.25
- w_neigh: bfloat16 [256, 256], replicated, may hold values from -1.25 to 1.25
- bias_vector: float32 [256], replicated, may hold values from -3 to 3
- pos_pairs: int32 [16, 256, 3], P('row', 'rep'), may hold values from 0 to 640, as said below
- neg_pairs: int32 [16, 256, 3], P('row', 'rep'), may hold values from 0 to 640, as said below
Outputs:
- embedding: bfloat16 [12288, 256], P(('row', 'rep'))
- pos_loss: float32 [16, 256, 128], P('row', 'rep')
- neg_loss: float32 [16, 256, 128], P('row', 'rep')
Inputs may be any that keep to these rules, and one draw needn't show every extreme that they name: `tile_live`: 1 marks a tile that counts (the adjacency holds nonzero values in every tile, live or not); every diagonal tile is live. `pos_pairs`: column 0 is below 6, column 1 below 8, column 2 at most 640, which is reached. `neg_pairs`: column 0 is below 6, column 1 below 8, column 2 at most 640, which is reached.
All inputs are finite; a program needn't handle non-finite values.
Results may differ from a plain program's by a relative error of at most 0.0037.
Values may be sent and summed in bfloat16 or wider, within the bound.
No kernel may reach another device: no remote copies, remote signals or barrier semaphores. Data moves between devices by JAX's collectives and lax.ppermute only.
A program may use at most 128 MiB of HBM per device.

v0:
```python
import math

import jax
import jax.numpy as jnp
from jax import lax
from jax.sharding import PartitionSpec as P

PAIR_ROWS = 128


def from_root(block, axis, holder):
    block = jnp.where(lax.axis_index(axis) == holder, block, jnp.zeros_like(block))
    return lax.psum(block, axis)


def project_rows(own_feats, summed, w_self, w_neigh, bias_vector):
    projected = jnp.dot(own_feats, w_self, preferred_element_type=jnp.float32)
    projected = projected + jnp.dot(
        summed.astype(jnp.bfloat16), w_neigh, preferred_element_type=jnp.float32
    )
    projected = projected + bias_vector
    scaled = projected * lax.rsqrt(jnp.mean(projected * projected, axis=-1, keepdims=True) + 1e-06)
    return scaled.astype(jnp.bfloat16)


def pair_losses(pairs, direction, embedding_block, key_stack):
    blocksize, channels = embedding_block.shape
    query_tiles = embedding_block.reshape(blocksize // PAIR_ROWS, PAIR_ROWS, channels)
    queries = query_tiles[pairs[:, 0]]
    zero_index = jnp.zeros((), jnp.int32)

    def take_keys(section_id, offset):
        return lax.dynamic_slice(
            key_stack, (section_id, offset, zero_index), (1, PAIR_ROWS, channels)
        )[0]

    key_rows = jax.vmap(take_keys)(pairs[:, 1], pairs[:, 2])
    scores = jnp.einsum(
        "pqf,pkf->pqk", queries, key_rows, preferred_element_type=jnp.float32
    ) / math.sqrt(channels)
    return jnp.mean(jax.nn.softplus(direction * scores), axis=-1)


def per_device(features, adjacency, tile_live, w_self, w_neigh, bias_vector, pos_pairs, neg_pairs):
    blocksize = features.shape[0]
    channels = features.shape[1]
    sections = tile_live.shape[1]
    replica = lax.axis_index("rep")
    first_section = replica * sections
    live_flags = tile_live[0]
    sources = [from_root(features, "row", first_section + section) for section in range(sections)]
    running = jnp.zeros((blocksize, channels), jnp.float32)
    for section in range(sections):
        tile_now = adjacency[:, section * blocksize : (section + 1) * blocksize]
        source_now = sources[section]
        product = jnp.dot(tile_now, source_now, preferred_element_type=jnp.float32)
        running = running + jnp.where(live_flags[section] > 0, product, 0.0)
    share = lax.psum_scatter(running, "rep", scatter_dimension=0, tiled=True)
    own_feats = lax.dynamic_slice_in_dim(features, replica * share.shape[0], share.shape[0], 0)
    embedding = project_rows(own_feats, share, w_self, w_neigh, bias_vector)
    embedding_block = lax.all_gather(embedding, "rep", axis=0, tiled=True)
    key_stack = jnp.stack(
        [from_root(embedding_block, "row", first_section + section) for section in range(sections)]
    )
    pos_loss = pair_losses(pos_pairs[0], -1.0, embedding_block, key_stack)
    neg_loss = pair_losses(neg_pairs[0], 1.0, embedding_block, key_stack)
    return (embedding, pos_loss[None], neg_loss[None])


def solution(mesh):
    return jax.shard_map(
        per_device,
        mesh=mesh,
        in_specs=(
            P("row", None),
            P("row", "rep"),
            P("row", "rep"),
            P(),
            P(),
            P(),
            P("row", "rep", None),
            P("row", "rep", None),
        ),
        out_specs=(P(("row", "rep"), None), P("row", "rep", None), P("row", "rep", None)),
        check_vma=False,
    )
```

profile of v0, /device:TPU:0, one launch (start us, length us, event | category | flops | bytes accessed | tf_op | source)
XLA Modules:
  0.0 386.1 jit_solution(10913288084373357945)
XLA Ops:
  16.8 103.8 %all-reduce.7.cloned.1.call-done = (bf16[768,256]{0,1:T(8,128)(2,1)}, bf16[768,256]{0,1:T(8,128)(2,1)}, bf16[768,256]{0,1:T(8,128)(2,1)}, bf16[768,256]{0,1:T(8,...) async-done(((bf16[768,256]{0,1:T(8,128)(2,1)}, bf16[768,256]{0,1:T(8,128)(2,1)}, ...) | async-done | bytes 3145744 | tf_op jit(solution)/shard_map/psum | solution.py:13
  120.6 2.0 convolution_select_fusion.7
  122.6 1.9 fusion.17
  124.6 1.9 fusion.16
  126.6 1.8 fusion.15
  128.4 1.8 fusion.14
  130.2 1.8 fusion.13
  132.0 1.8 fusion.12
  133.8 2.7 fusion.11
  136.9 16.2 %reduce-scatter.2.cloned.1.call-done = f32[384,256]{0,1:T(8,128)} async-done(((f32[768,256]{0,1:T(8,128)}), f32[384,256]{0,1:T(8,128)}) %reduce-scatter.2.cloned.1.call-update) | async-done | bytes 393232 | tf_op jit(solution)/shard_map/reduce_scatter | solution.py:58
  154.4 7.3 %all_gather.3 = bf16[768,256]{0,1:T(8,128)(2,1)S(1)} all-gather(bf16[384,256]{0,1:T(8,128)(2,1)S(1)} %multiply_convert_fusion), channel_id=1, replica_groups=mesh['row'=16,'rep'=2] {'rep'}, dimensions={0}, use_global_device_ids=true | all-gather | bytes 589824 | tf_op jit(solution)/shard_map/all_gather | solution.py:61
  164.5 6.6 %gather_fusion.2 = bf16[128,128,256]{2,1,0:T(8,128)(2,1)} fusion(bf16[6,128,256]{2,1,0:T(8,128)(2,1)S(1)} %bitcast.57, s32[1024]{0:T(1024)S(1)} %get-tuple-element.55), kind=kCustom, calls=%fused_computation.2 | custom fusion | bytes 16777728 | tf_op jit(solution)/shard_map/gather | solution.py:29
  171.1 6.6 %gather_fusion = bf16[128,128,256]{2,1,0:T(8,128)(2,1)} fusion(bf16[6,128,256]{2,1,0:T(8,128)(2,1)S(1)} %bitcast.58, s32[1024]{0:T(1024)S(1)} %get-tuple-element.56), kind=kCustom, calls=%fused_computation | custom fusion | bytes 16777728 | tf_op jit(solution)/shard_map/gather | solution.py:29
  177.7 91.3 %all-reduce.5.cloned.1.call-done = (bf16[1,768,256]{1,2,0:T(8,128)(2,1)}, bf16[1,768,256]{1,2,0:T(8,128)(2,1)}, bf16[1,768,256]{1,2,0:T(8,128)(2,1)}, bf16[1,768...) async-done(((bf16[1,768,256]{1,2,0:T(8,128)(2,1)}, ...) | async-done | bytes 3145744 | tf_op jit(solution)/shard_map/psum | solution.py:13
  270.7 1.8 constant_dynamic-update-slice_fusion.6
  274.2 1.8 constant_dynamic-update-slice_fusion.4
  277.8 1.8 constant_dynamic-update-slice_fusion.2
  279.6 1.8 constant_dynamic-update-slice_fusion.1
  281.4 1.8 constant_dynamic-update-slice_fusion
  283.1 4.1 %copy.33 = bf16[8,768,256]{2,0,1:T(8,128)(2,1)S(1)} copy(bf16[8,768,256]{1,2,0:T(8,128)(2,1)} %constant_dynamic-update-slice_fusion) | data formatting | bytes 6291456 | tf_op jit(solution)/shard_map/stack | solution.py:62
  287.3 30.8 %gather_fusion.3 = bf16[128,128,256]{2,0,1:T(8,128)(2,1)} fusion(bf16[8,768,256]{2,0,1:T(8,128)(2,1)S(1)} %copy.33, s32[128]{0:T(128)S(1)} %get-tuple-element.41), kind=kCustom, calls=%fused_computation.3 | custom fusion | bytes 16778752 | tf_op jit(solution)/shard_map/vmap()/gather | solution.py:33
  318.0 14.7 %fusion.1 = f32[128,128]{1,0:T(8,128)S(1)} fusion(bf16[128,128,256]{2,1,0:T(8,128)(2,1)} %gather_fusion.2, bf16[128,128,256]{2,0,1:T(8,128)(2,1)} %gather_fusion.3), kind=kOutput, calls=%fused_computation.7 | convolution fusion | flops 1090502656 | bytes 16842752 | tf_op jit(solution)/shard_map/pqf,pkf->pqk/dot_general | solution.py:38
  333.4 30.6 %gather_fusion.1 = bf16[128,128,256]{2,0,1:T(8,128)(2,1)} fusion(bf16[8,768,256]{2,0,1:T(8,128)(2,1)S(1)} %copy.33, s32[128]{0:T(128)S(1)} %get-tuple-element.43), kind=kCustom, calls=%fused_computation.1 | custom fusion | bytes 16778752 | tf_op jit(solution)/shard_map/vmap()/gather | solution.py:33
  364.0 14.7 %fusion = f32[128,128]{1,0:T(8,128)S(1)} fusion(bf16[128,128,256]{2,1,0:T(8,128)(2,1)} %gather_fusion, bf16[128,128,256]{2,0,1:T(8,128)(2,1)} %gather_fusion.1), kind=kOutput, calls=%fused_computation.6 | convolution fusion | flops 1090502656 | bytes 16842752 | tf_op jit(solution)/shard_map/pqf,pkf->pqk/dot_general | solution.py:38
  (50 shorter events, 15.6 us)
Async XLA Ops:
  7.2 145.9 %copy-start = (bf16[256,256]{1,0:T(8,128)(2,1)S(1)}, bf16[256,256]{1,0:T(8,128)(2,1)}, u32[]{:S(2)}) copy-start(bf16[256,256]{1,0:T(8,128)(2,1)} %param.12) | copy-start | bytes 393220
  7.2 113.4 %all-reduce.7.cloned.1.call-start = ((), (), s32[]{:S(2)}) async-start(), calls=%async_computation.3 | async-start | bytes 6291456 | tf_op jit(solution)/shard_map/psum | solution.py:13
  10.2 142.9 %reduce-scatter.2.cloned.1.call-start = ((), (), s32[]{:S(2)}) async-start(), calls=%async_computation.1 | async-start | bytes 1179648 | tf_op jit(solution)/shard_map/reduce_scatter | solution.py:58
  120.6 5.9 %copy-start.7 = (bf16[768,256]{0,1:T(8,128)(2,1)S(1)}, bf16[768,256]{0,1:T(8,128)(2,1)}, u32[]{:S(2)}) copy-start(bf16[768,256]{0,1:T(8,128)(2,1)} %get-tuple-element.20) | copy-start | bytes 1179652
  120.6 7.8 %copy-start.6 = (bf16[768,256]{0,1:T(8,128)(2,1)S(1)}, bf16[768,256]{0,1:T(8,128)(2,1)}, u32[]{:S(2)}) copy-start(bf16[768,256]{0,1:T(8,128)(2,1)} %get-tuple-element.21) | copy-start | bytes 1179652
  120.6 9.6 %copy-start.5 = (bf16[768,256]{0,1:T(8,128)(2,1)S(1)}, bf16[768,256]{0,1:T(8,128)(2,1)}, u32[]{:S(2)}) copy-start(bf16[768,256]{0,1:T(8,128)(2,1)} %get-tuple-element.22) | copy-start | bytes 1179652
  122.6 9.4 %copy-start.4 = (bf16[768,256]{0,1:T(8,128)(2,1)S(1)}, bf16[768,256]{0,1:T(8,128)(2,1)}, u32[]{:S(2)}) copy-start(bf16[768,256]{0,1:T(8,128)(2,1)} %get-tuple-element.23) | copy-start | bytes 1179652
  124.6 9.3 %copy-start.3 = (bf16[768,256]{0,1:T(8,128)(2,1)S(1)}, bf16[768,256]{0,1:T(8,128)(2,1)}, u32[]{:S(2)}) copy-start(bf16[768,256]{0,1:T(8,128)(2,1)} %get-tuple-element.24) | copy-start | bytes 1179652
  126.5 10.1 %copy-start.2 = (bf16[768,256]{1,0:T(8,128)(2,1)S(1)}, bf16[768,256]{1,0:T(8,128)(2,1)}, u32[]{:S(2)}) copy-start(bf16[768,256]{1,0:T(8,128)(2,1)} %param.8) | copy-start | bytes 1179652
  126.5 10.1 %copy-start.8 = (bf16[256,256]{1,0:T(8,128)(2,1)S(1)}, bf16[256,256]{1,0:T(8,128)(2,1)}, u32[]{:S(2)}) copy-start(bf16[256,256]{1,0:T(8,128)(2,1)} %param.11) | copy-start | bytes 393220
  126.6 26.5 %copy-start.11 = (f32[256]{0:T(256)S(1)}, f32[256]{0:T(256)}, u32[]{:S(2)}) copy-start(f32[256]{0:T(256)} %param.13) | copy-start | bytes 3076
  132.0 31.4 %copy-start.9 = (s32[1,128,3]{1,0,2:T(1,128)S(1)}, s32[1,128,3]{1,0,2:T(1,128)}, u32[]{:S(2)}) copy-start(s32[1,128,3]{1,0,2:T(1,128)} %param.15) | copy-start | bytes 4612
  132.0 31.4 %copy-start.10 = (s32[1,128,3]{1,0,2:T(1,128)S(1)}, s32[1,128,3]{1,0,2:T(1,128)}, u32[]{:S(2)}) copy-start(s32[1,128,3]{1,0,2:T(1,128)} %param.14) | copy-start | bytes 4612
  136.5 132.4 %all-reduce.5.cloned.1.call-start = ((), (), s32[]{:S(2)}) async-start(), calls=%async_computation.2 | async-start | bytes 6291456 | tf_op jit(solution)/shard_map/psum | solution.py:13
  364.0 15.4 %copy-start.1 = (bf16[256,256]{1,0:T(8,128)(2,1)S(1)}, bf16[256,256]{1,0:T(8,128)(2,1)}, u32[]{:S(2)}) copy-start(bf16[256,256]{1,0:T(8,128)(2,1)} %param.12) | copy-start | bytes 393220
Sparse Core Ops, SparseCore 0:
  12.5 108.0 all-reduce.6
  136.7 16.3 reduce-scatter.1
  163.5 105.3 all-reduce.4
where the time goes:
time: 394 us; the launch traced here: 386 us
  waiting for transfers between devices  211 us (54%)
  local copies, waits for them, and re-layouts  96.7 us (25%)
  matrix products  46.7 us (12%)
  between operations  19.3 us (5%)
  blocking collectives  7.3 us (2%)
  other arithmetic  4.73 us (1%)
    psum x2, waiting for transfers between devices, from_root(): return lax.psum(block, axis)  195 us
    gather x2, local copies, waits for them, and re-layouts, take_keys(): lax.dynamic_slice(key_stack, (section_id, offset, zero_index), (1, PAIR_R...  61.4 us
    dot_general x2, matrix products, pair_losses(): jnp.einsum('pqf,pkf->pqk', queries, key_rows, preferred_element_type=jnp....  29.4 us
    reduce_scatter x1, waiting for transfers between devices, per_device(): share = lax.psum_scatter(running, 'rep', scatter_dimension=0, tiled=True)  16.2 us
    dot_general x8, matrix products, per_device(): product = jnp.dot(tile_now, source_now, preferred_element_type=jnp.float32)  15.7 us
    unnamed x35, local copies, waits for them, and re-layouts  14.5 us
    gather x2, local copies, waits for them, and re-layouts, pair_losses(): queries = query_tiles[pairs[:, 0]]  13.2 us
  transfers between devices with their start and end apart: 3, of which 3 were waited for; matrix products, arithmetic and copies ran while one was open for 4% of the time, Pallas kernels for 0%

commit v1 on v0

v1 whole, which is shorter than its diff:
```python
import functools
import math

import jax
import jax.numpy as jnp
from jax import lax
from jax.experimental import pallas as pl
from jax.experimental.pallas import tpu as pltpu
from jax.sharding import PartitionSpec as P

PAIR_ROWS = 128
EDGE = 8
UNROLL = 8
WIDE = 256


def permute(block, pairs, n_rep):
    return lax.ppermute(
        block, ("row", "rep"), [(a[0] * n_rep + a[1], b[0] * n_rep + b[1]) for a, b in pairs]
    )


def aggregate_kernel(rows_of, members, fetch, sections, has_tiles, has_previous, live_ref, *refs):
    n_pieces = sum(len(rows) for rows in rows_of)
    piece_refs, refs = refs[:n_pieces], refs[n_pieces:]
    previous_ref, refs = (refs[0], refs[1:]) if has_previous else (None, refs)
    if has_tiles:
        tile_refs, (out_ref,) = refs[: len(members)], refs[len(members) :]
    else:
        adjacency_ref, out_ref = refs[:2]
        fetch_refs, (tiles, sem) = refs[2 : 2 + len(fetch)], refs[2 + len(fetch) :]
        tile_refs = [tiles.at[b] for b in range(len(members))]
    member = lax.rem(lax.axis_index("row"), sections)
    odd = member & 1

    def section(slot):
        return member ^ jnp.where(odd > 0, slot[1], slot[0])

    places = [section(slot) for slot in members]
    blocksize = out_ref.shape[0]
    copies = []
    if not has_tiles:
        for slot, target in zip(list(members) + fetch, list(tile_refs) + list(fetch_refs)):
            column = pl.multiple_of(section(slot) * blocksize, PAIR_ROWS)
            copy = pltpu.make_async_copy(
                adjacency_ref.at[:, pl.ds(column, blocksize)], target, sem.at[len(copies)]
            )
            pl.when(live_ref[0, section(slot)] > 0)(copy.start)
            copies.append(copy)
    if has_previous:
        out_ref[...] = previous_ref[...]
    else:
        out_ref[...] = jnp.zeros_like(out_ref)
    at = 0
    for b, rows in enumerate(rows_of):
        pieces = piece_refs[at : at + len(rows)]
        at += len(rows)

        @pl.when(live_ref[0, places[b]] > 0)
        def _():
            if not has_tiles:
                copies[b].wait()
            for piece, to in zip(pieces, rows):
                out_ref[...] += jnp.dot(
                    tile_refs[b][:, to : to + piece.shape[0]],
                    piece[...],
                    preferred_element_type=jnp.float32,
                )

    for slot, copy in zip(fetch, copies[len(members) :]):
        pl.when(live_ref[0, section(slot)] > 0)(copy.wait)


def vmem(count):
    return [pl.BlockSpec(memory_space=pltpu.VMEM)] * count


def aggregate(tile_live, adjacency, blocks, members, previous, tiles=None, fetch=()):
    blocksize = adjacency.shape[0]
    channels = blocks[0][0][0].shape[1]
    fetch = list(fetch)
    pieces = [piece for block in blocks for piece, _ in block]
    rows_of = [[to for _, to in block] for block in blocks]
    extra = [] if previous is None else [previous]
    extra_tiles = [] if tiles is None else list(tiles)
    tile = jax.ShapeDtypeStruct((blocksize, blocksize), adjacency.dtype)
    n_loads = len(members) + len(fetch)
    out = pl.pallas_call(
        functools.partial(
            aggregate_kernel,
            rows_of,
            members,
            fetch,
            adjacency.shape[1] // blocksize,
            tiles is not None,
            previous is not None,
        ),
        in_specs=[pl.BlockSpec(memory_space=pltpu.SMEM)]
        + vmem(len(pieces) + len(extra) + len(extra_tiles))
        + ([pl.BlockSpec(memory_space=pl.ANY)] if tiles is None else []),
        out_specs=vmem(1 + len(fetch)),
        out_shape=[jax.ShapeDtypeStruct((blocksize, channels), jnp.float32)] + [tile] * len(fetch),
        scratch_shapes=[
            pltpu.VMEM((len(members), blocksize, blocksize), adjacency.dtype),
            pltpu.SemaphoreType.DMA((n_loads,)),
        ]
        if tiles is None
        else [],
        compiler_params=pltpu.CompilerParams(
            vmem_limit_bytes=(44 if tiles is None else 8) * 1024 * 1024
        ),
    )(tile_live, *pieces, *extra, *(extra_tiles if tiles is not None else [adjacency]))
    return out[0], out[1:]


def score_kernel(rows_of, which, has_previous, code_ref, ends_ref, emb_ref, *refs):
    n_pieces = sum(len(rows) for rows in rows_of)
    piece_refs, refs = refs[:n_pieces], refs[n_pieces:]
    previous_refs, refs = (refs[:2], refs[2:]) if has_previous else (None, refs)
    pos_ref, neg_ref, scores, losses = refs
    blocksize, channels = emb_ref.shape
    n_pairs = pos_ref.shape[0]
    n_tiles = blocksize // PAIR_ROWS
    if has_previous:
        losses[:n_pairs, :] = previous_refs[0][...]
        losses[n_pairs:, :] = previous_refs[1][...]
    else:
        losses[...] = jnp.zeros_like(losses)
    scores[:, len(rows_of) * blocksize :, :] = jnp.zeros((n_tiles, EDGE, PAIR_ROWS), jnp.float32)
    at = 0
    for b, rows in enumerate(rows_of):
        for piece, to in zip(piece_refs[at : at + len(rows)], rows):
            first = b * blocksize + to
            for t in range(0, n_tiles, WIDE // PAIR_ROWS):
                product = lax.dot_general(
                    piece[...],
                    emb_ref[t * PAIR_ROWS : t * PAIR_ROWS + WIDE, :],
                    (((1,), (1,)), ((), ())),
                    preferred_element_type=jnp.float32,
                )
                for u in range(WIDE // PAIR_ROWS):
                    scores[t + u, first : first + piece.shape[0], :] = product[
                        :, u * PAIR_ROWS : (u + 1) * PAIR_ROWS
                    ]
        at += len(rows)

    row_of = lax.broadcasted_iota(jnp.int32, (EDGE, PAIR_ROWS), 0)
    scale = math.log2(math.e) / math.sqrt(channels)
    first_pair, end_pair = ends_ref[which], ends_ref[which + 1]

    def one_pair(at):
        code = code_ref[at]
        query = code & 7
        first = lax.shift_right_logical(code, 3) & 0x1FFF
        out_row = lax.shift_right_logical(code, 16)
        factor = jnp.where(out_row >= n_pairs, scale, -scale)
        base = pl.multiple_of(first & ~(EDGE - 1), EDGE)
        shift = first & (EDGE - 1)
        window = scores[query, pl.ds(base, PAIR_ROWS + EDGE), :]
        edge = jnp.where(row_of >= shift, window[:EDGE], window[PAIR_ROWS:])
        window = jnp.concatenate([edge, window[EDGE:PAIR_ROWS]], axis=0)
        terms = 1.0 + jnp.exp2(window * factor)
        quarter = PAIR_ROWS // 4
        product = (terms[:quarter] * terms[quarter : 2 * quarter]) * (
            terms[2 * quarter : 3 * quarter] * terms[3 * quarter :]
        )
        return out_row, jnp.sum(jnp.log(product), axis=0, keepdims=True) * (1.0 / PAIR_ROWS)

    def step(i, carry):
        start = first_pair + i * UNROLL
        results = [one_pair(jnp.minimum(start + u, end_pair - 1)) for u in range(UNROLL)]
        for out_row, loss in results:
            losses[pl.ds(out_row, 1), :] = loss
        return carry

    lax.fori_loop(0, lax.div(end_pair - first_pair + (UNROLL - 1), UNROLL), step, 0)
    pos_ref[...] = losses[:n_pairs, :]
    neg_ref[...] = losses[n_pairs:, :]


def score_pairs(codes, ends, which, embedding_block, blocks, n_pairs, previous):
    blocksize, channels = embedding_block.shape
    n_rows = len(blocks) * blocksize
    loss = jax.ShapeDtypeStruct((n_pairs, PAIR_ROWS), jnp.float32)
    pieces = [piece for block in blocks for piece, _ in block]
    rows_of = [[to for _, to in block] for block in blocks]
    extra = [] if previous is None else list(previous)
    return pl.pallas_call(
        functools.partial(score_kernel, rows_of, which, previous is not None),
        in_specs=[pl.BlockSpec(memory_space=pltpu.SMEM)] * 2 + vmem(1 + len(pieces) + len(extra)),
        out_specs=vmem(2),
        scratch_shapes=[
            pltpu.VMEM((blocksize // PAIR_ROWS, n_rows + EDGE, PAIR_ROWS), jnp.float32),
            pltpu.VMEM((2 * n_pairs, PAIR_ROWS), jnp.float32),
        ],
        out_shape=[loss, loss],
        compiler_params=pltpu.CompilerParams(vmem_limit_bytes=24 * 1024 * 1024),
    )(codes, ends, embedding_block, *pieces, *extra)


def order_pairs(pairs, member, sets, blocksize):
    n_all = pairs.shape[0]
    place = pairs[:, 1] ^ member
    in_set = jnp.zeros_like(place)
    at = jnp.zeros_like(place)
    for c, members in enumerate(sets):
        for i, (even, odd) in enumerate(members):
            here = place == jnp.where(member & 1 > 0, odd, even)
            in_set = jnp.where(here, c, in_set)
            at = jnp.where(here, i, at)
    index = jnp.arange(n_all, dtype=jnp.int32)
    code = ((index << 16) | ((at * blocksize + pairs[:, 2]) << 3)) | pairs[:, 0]
    sort_by = in_set * n_all + index
    rank = jnp.sum((sort_by[None, :] < sort_by[:, None]).astype(jnp.int32), axis=1)
    codes = jnp.sum(jnp.where(rank[None, :] == index[:, None], code[None, :], 0), axis=1)
    levels = jnp.arange(len(sets) + 1, dtype=jnp.int32)
    ends = jnp.sum((in_set[None, :] < levels[:, None]).astype(jnp.int32), axis=1)
    return codes, ends


class Spread:
    def __init__(self, n_row, n_rep, sections):
        self.n_row, self.n_rep, self.sections = n_row, n_rep, sections
        self.groups = n_row // sections
        self.rep = lax.axis_index("rep")
        row = lax.axis_index("row")
        self.group, self.member = row // sections, row % sections
        self.everyone = [(r, p) for r in range(n_row) for p in range(n_rep)]
        self.halved = n_rep == 2 and self.groups == 2 and sections == 8
        if self.halved:
            self.slots = [(0, 0), (1, 1), (2, 4), (5, 3), (4, 2), (3, 5), (6, 6), (7, 7)]
            self.sets = [[0, 1], [2, 3, 4, 5], [6], [7]]
        else:
            self.slots = [(j, j) for j in range(sections)]
            self.sets = [list(range(sections))]
        self.members = [[self.slots[slot] for slot in members] for members in self.sets]

    def flip(self, block, stride):
        return permute(
            block, [((r, p), (r ^ stride, p)) for r, p in self.everyone], self.n_rep
        )

    def flip_either(self, block, even, odd):
        return permute(
            block,
            [((r, p), (r ^ (odd if r & 1 else even), p)) for r, p in self.everyone],
            self.n_rep,
        )

    def to_holder(self, block):
        return permute(
            block, [((r, p), (r, r & 1)) for r, p in self.everyone if p != r & 1], self.n_rep
        )

    def from_holder(self, block):
        return permute(
            block, [((r, p), (r, 1 - p)) for r, p in self.everyone if p == r & 1], self.n_rep
        )

    def run_halved(self, held, own, consume):
        n = self.sections
        half = own[0].shape[0]
        across = [
            ((r, p), ((r + n) % self.n_row, r // n)) for r, p in self.everyone if p == r & 1
        ]
        start, near, first, second = [], [], [], []
        came = [permute(part, across, self.n_rep) for part in held]
        for own_part, came_part in zip(own, came):
            part = jnp.where(self.group == self.rep, own_part, came_part)
            start.append(part)
            first.append(self.flip_either(part, 2, 4))
            second.append(self.flip_either(part, 4, 2))
            near.append(self.flip(part, 1))

        def whole(parts):
            return [(part, i * half) for i, part in enumerate(parts)]

        def near_of(parts):
            return [self.flip(part, 1) for part in parts]

        done = consume(0, [whole(start), whole(near)], None)
        first[1], second[1], done = lax.optimization_barrier((first[1], second[1], done))
        third = [self.flip_either(part, 4, 2) for part in first]
        done = consume(
            1,
            [whole(x) for parts in (first, second) for x in (parts, near_of(parts))],
            done,
        )
        third[1], done = lax.optimization_barrier((third[1], done))
        near_third = near_of(third)
        done = consume(2, [whole(third)], done)
        return consume(3, [whole(near_third)], done)

    def run_whole(self, block, consume):
        start = block
        for d in range(1, self.groups):
            came = permute(
                block,
                [
                    ((p * self.sections + m, p), (((p + d) % self.groups) * self.sections + m, p))
                    for p in range(self.n_rep)
                    for m in range(self.sections)
                ],
                self.n_rep,
            )
            start = jnp.where(self.group == (self.rep + d) % self.groups, came, start)
        blocks = {0: start}
        for b in reversed(range(self.sections.bit_length() - 1)):
            for j in list(blocks):
                blocks[j ^ (1 << b)] = self.flip(blocks[j], 1 << b)
        return consume(0, [[(blocks[j], 0)] for j in range(self.sections)], None)


def per_device(
    n_row, n_rep, features, adjacency, tile_live, w_self, w_neigh, bias_vector, pos_pairs, neg_pairs
):
    blocksize = features.shape[0]
    sections = tile_live.shape[1]
    n_pairs = pos_pairs.shape[1]
    share = blocksize // n_rep
    spread = Spread(n_row, n_rep, sections)
    rep, sets = spread.rep, spread.members

    fetched = {}

    def add_tiles(which, blocks, earlier):
        members = sets[which]
        last = [slot for later in sets[2:] for slot in later] if which == 1 else []
        tiles = [fetched[slot] for slot in members] if members[0] in fetched else None
        total, more = aggregate(tile_live, adjacency, blocks, members, earlier, tiles, last)
        fetched.update(zip(last, more))
        return total

    if spread.halved:
        parts = [features[:share], features[share:]]
        partial = spread.run_halved(parts, parts, add_tiles)
    else:
        partial = spread.run_whole(features, add_tiles)

    codes, ends = order_pairs(
        jnp.concatenate([pos_pairs[0], neg_pairs[0]], axis=0), spread.member, sets, blocksize
    )
    def embed(feats, summed):
        projected = jnp.dot(feats, w_self, preferred_element_type=jnp.float32) + bias_vector
        projected = projected + jnp.dot(
            summed.astype(jnp.bfloat16), w_neigh, preferred_element_type=jnp.float32
        )
        scale = lax.rsqrt(jnp.mean(projected * projected, axis=-1, keepdims=True) + 1e-06)
        return (projected * scale).astype(jnp.bfloat16)

    if spread.halved:
        held = []
        for i, feats in enumerate(parts):
            mine = partial[i * share : (i + 1) * share]
            other = spread.to_holder(mine.astype(jnp.bfloat16))
            held.append(embed(feats, mine + other.astype(jnp.float32)))
    else:
        own_feats = lax.dynamic_slice_in_dim(features, rep * share, share, 0)
        embedding = embed(own_feats, lax.psum_scatter(partial, "rep", scatter_dimension=0, tiled=True))

    def score(queries, which, blocks, earlier):
        return score_pairs(codes, ends, which, queries, blocks, n_pairs, earlier)

    if spread.halved:
        holder = rep == spread.member & 1
        own = [jnp.where(holder, part, spread.from_holder(part)) for part in held]
        block = jnp.concatenate(own, axis=0)
        embedding = jnp.where(rep == 0, own[0], own[1])
        losses = spread.run_halved(held, own, functools.partial(score, block))
    else:
        block = lax.all_gather(embedding, "rep", axis=0, tiled=True)
        losses = spread.run_whole(block, functools.partial(score, block))
    return (embedding, losses[0][None], losses[1][None])


def solution(mesh):
    return jax.shard_map(
        functools.partial(per_device, mesh.shape["row"], mesh.shape["rep"]),
        mesh=mesh,
        in_specs=(
            P("row", None),
            P("row", "rep"),
            P("row", "rep"),
            P(),
            P(),
            P(),
            P("row", "rep", None),
            P("row", "rep", None),
        ),
        out_specs=(P(("row", "rep"), None), P("row", "rep", None), P("row", "rep", None)),
        check_vma=False,
    )
```

time: 394 us -> 86.9 us (0.22)
  the two profiles are of different devices: /device:TPU:0 before, /device:TPU:3 now
where the time goes in v1:
time: 86.9 us; the launch traced here: 86.4 us
  starting transfers between devices  44.4 us (51%)
  waiting for transfers between devices  23.6 us (27%)
  Pallas kernels  12.4 us (14%)
  other arithmetic  2.75 us (3%)
  local copies, waits for them, and re-layouts  1.1 us (1%)
  between operations  1.09 us (1%)
  matrix products  1.06 us (1%)
    ppermute x36, starting transfers between devices, permute(): lax.ppermute(block, ('row', 'rep'), [(a[0] * n_rep + a[1], b[0] * n_rep +...  44.4 us
    ppermute x36, waiting for transfers between devices, permute(): lax.ppermute(block, ('row', 'rep'), [(a[0] * n_rep + a[1], b[0] * n_rep +...  23.6 us
    pallas_call x4, Pallas kernels, score_pairs(): pl.pallas_call(functools.partial(score_kernel, rows_of, which, previous i...  9.92 us
    pallas_call x4, Pallas kernels, aggregate(): pl.pallas_call(functools.partial(aggregate_kernel, rows_of, members, fetc...  2.5 us
  transfers between devices with their start and end apart: 36, of which 12 were waited for; matrix products, arithmetic and copies ran while one was open for 3% of the time, Pallas kernels for 11%

profile of v1, /device:TPU:3, one launch (start us, length us, event | category | flops | bytes accessed | tf_op | source)
XLA Modules:
  0.0 86.4 jit_solution(4186451140985653593)
XLA Ops:
  1.7 4.2 %collective-permute-start.4 = (bf16[384,256]{1,0:T(8,128)(2,1)S(1)}, bf16[384,256]{1,0:T(8,128)(2,1)S(1)}, u32[]{:S(2)}, u32[]{:S(2)}) collective-permute-start(bf16[384,256]{1,0:T(8,128)(2,1)S(1)} %slice.22), channel_id=1, source_target_pairs={{0,16},{3,18},{4,20},{7,22},{8,24},{11,26},{12,28},{15,30},{16,1},... | collective-permute-start | bytes 589832 | tf_op jit(solution)/shard_map/ppermute | solution.py:18
  5.9 5.5 %collective-permute-done.4 = bf16[384,256]{1,0:T(8,128)(2,1)S(1)} collective-permute-done((bf16[384,256]{1,0:T(8,128)(2,1)S(1)}, bf16[384,256]{1,0:T(8,128)(2,1)S(1)}, u32[]{:S(2)}, u32[]{:S(2)}) %collective-permute-start.4) | collective-permute-done | bytes 196640 | tf_op jit(solution)/shard_map/ppermute | solution.py:18
  12.5 2.8 %collective-permute-start = (bf16[384,256]{1,0:T(8,128)(2,1)S(1)}, bf16[384,256]{1,0:T(8,128)(2,1)S(1)}, u32[]{:S(2)}, u32[]{:S(2)}) collective-permute-start(bf16[384,256]{1,0:T(8,128)(2,1)S(1)} %get-tuple-element.58), channel_id=1, source_target_pairs={{0,16},{3,18},{4,20},{7,22},{8,24},{11,26},{12,28},{15,30},{16,1},... | collective-permute-start | bytes 589832 | tf_op jit(solution)/shard_map/ppermute | solution.py:18
  16.4 2.3 %collective-permute-start.5 = (bf16[384,256]{1,0:T(8,128)(2,1)S(1)}, bf16[384,256]{1,0:T(8,128)(2,1)S(1)}, u32[]{:S(2)}, u32[]{:S(2)}) collective-permute-start(bf16[384,256]{1,0:T(8,128)(2,1)S(1)} %get-tuple-element.57.refs_1_), channel_id=1, source_target_pairs={{0,4},{1,5},{2,10},{3,11},{4,0},{5,1},{6,14},{7,15},{8,12},{9,13},... | collective-permute-start | bytes 589832 | tf_op jit(solution)/shard_map/ppermute | solution.py:18
  19.9 2.3 %collective-permute-done = bf16[384,256]{1,0:T(8,128)(2,1)S(1)} collective-permute-done((bf16[384,256]{1,0:T(8,128)(2,1)S(1)}, bf16[384,256]{1,0:T(8,128)(2,1)S(1)}, u32[]{:S(2)}, u32[]{:S(2)}) %collective-permute-start) | collective-permute-done | bytes 196640 | tf_op jit(solution)/shard_map/ppermute | solution.py:18
  22.3 3.3 %collective-permute-start.7 = (bf16[384,256]{1,0:T(8,128)(2,1)S(1)}, bf16[384,256]{1,0:T(8,128)(2,1)S(1)}, u32[]{:S(2)}, u32[]{:S(2)}) collective-permute-start(bf16[384,256]{1,0:T(8,128)(2,1)S(1)} %broadcast_select_fusion.3.refs_0_), channel_id=1, source_target_pairs={{0,2},{1,3},{2,0},{3,1},{4,6},{5,7},{6,4},{7,5},{8,10},{9,11},{10,... | collective-permute-start | bytes 589832 | tf_op jit(solution)/shard_map/ppermute | solution.py:18
  25.6 1.3 %collective-permute-start.12 = (bf16[384,256]{1,0:T(8,128)(2,1)S(1)}, bf16[384,256]{1,0:T(8,128)(2,1)S(1)}, u32[]{:S(2)}, u32[]{:S(2)}) collective-permute-start(bf16[384,256]{1,0:T(8,128)(2,1)S(1)} %broadcast_select_fusion.3.refs_0_), channel_id=1, source_target_pairs={{0,8},{1,9},{2,6},{3,7},{4,12},{5,13},{6,2},{7,3},{8,0},{9,1},{10,... | collective-permute-start | bytes 589832 | tf_op jit(solution)/shard_map/ppermute | solution.py:18
  29.0 2.9 %collective-permute-start.14 = (bf16[384,256]{1,0:T(8,128)(2,1)S(1)}, bf16[384,256]{1,0:T(8,128)(2,1)S(1)}, u32[]{:S(2)}, u32[]{:S(2)}) collective-permute-start(bf16[384,256]{1,0:T(8,128)(2,1)S(1)} %collective-permute-done.6.refs_5_), channel_id=1, source_target_pairs={{0,2},{1,3},{2,0},{3,1},{4,6},{5,7},{6,4},{7,5},{8,10},{9,11},{10,... | collective-permute-start | bytes 589832 | tf_op jit(solution)/shard_map/ppermute | solution.py:18
  31.9 1.5 %collective-permute-start.10 = (bf16[384,256]{1,0:T(8,128)(2,1)S(1)}, bf16[384,256]{1,0:T(8,128)(2,1)S(1)}, u32[]{:S(2)}, u32[]{:S(2)}) collective-permute-start(bf16[384,256]{1,0:T(8,128)(2,1)S(1)} %collective-permute-done.1.refs_0_), channel_id=1, source_target_pairs={{0,2},{1,3},{2,0},{3,1},{4,6},{5,7},{6,4},{7,5},{8,10},{9,11},{10,... | collective-permute-start | bytes 589832 | tf_op jit(solution)/shard_map/ppermute | solution.py:18
  36.8 2.1 %collective-permute-start.15 = (bf16[384,256]{1,0:T(8,128)(2,1)S(1)}, bf16[384,256]{1,0:T(8,128)(2,1)S(1)}, u32[]{:S(2)}, u32[]{:S(2)}) collective-permute-start(bf16[384,256]{1,0:T(8,128)(2,1)S(1)} %collective-permute-done.9.refs_1_), channel_id=1, source_target_pairs={{0,2},{1,3},{2,0},{3,1},{4,6},{5,7},{6,4},{7,5},{8,10},{9,11},{10,... | collective-permute-start | bytes 589832 | tf_op jit(solution)/shard_map/ppermute | solution.py:18
  43.8 3.6 %collective-permute-done.18 = bf16[384,256]{1,0:T(8,128)(2,1)S(1)} collective-permute-done((bf16[384,256]{1,0:T(8,128)(2,1)S(1)}, bf16[384,256]{1,0:T(8,128)(2,1)S(1)}, u32[]{:S(2)}, u32[]{:S(2)}) %collective-permute-start.18) | collective-permute-done | bytes 196640 | tf_op jit(solution)/shard_map/ppermute | solution.py:18
  47.9 1.5 %collective-permute-start.19 = (bf16[384,256]{1,0:T(8,128)(2,1)S(1)}, bf16[384,256]{1,0:T(8,128)(2,1)S(1)}, u32[]{:S(2)}, u32[]{:S(2)}) collective-permute-start(bf16[384,256]{1,0:T(8,128)(2,1)S(1)} %multiply_convert_fusion), channel_id=1, source_target_pairs={{0,1},{3,2},{4,5},{7,6},{8,9},{11,10},{12,13},{15,14},{16,17},{19,... | collective-permute-start | bytes 589832 | tf_op jit(solution)/shard_map/ppermute | solution.py:18
  49.4 1.9 %collective-permute-start.24 = (bf16[384,256]{1,0:T(8,128)(2,1)S(1)}, bf16[384,256]{1,0:T(8,128)(2,1)S(1)}, u32[]{:S(2)}, u32[]{:S(2)}) collective-permute-start(bf16[384,256]{1,0:T(8,128)(2,1)S(1)} %multiply_convert_fusion), channel_id=1, source_target_pairs={{0,16},{3,18},{4,20},{7,22},{8,24},{11,26},{12,28},{15,30},{16,1},... | collective-permute-start | bytes 589832 | tf_op jit(solution)/shard_map/ppermute | solution.py:18
  51.8 1.3 %collective-permute-start.17 = (bf16[384,256]{1,0:T(8,128)(2,1)S(1)}, bf16[384,256]{1,0:T(8,128)(2,1)S(1)}, u32[]{:S(2)}, u32[]{:S(2)}) collective-permute-start(bf16[384,256]{1,0:T(8,128)(2,1)S(1)} %multiply_convert_fusion.1), channel_id=1, source_target_pairs={{0,1},{3,2},{4,5},{7,6},{8,9},{11,10},{12,13},{15,14},{16,17},{19,... | collective-permute-start | bytes 589832 | tf_op jit(solution)/shard_map/ppermute | solution.py:18
  53.1 1.9 %collective-permute-start.20 = (bf16[384,256]{1,0:T(8,128)(2,1)S(1)}, bf16[384,256]{1,0:T(8,128)(2,1)S(1)}, u32[]{:S(2)}, u32[]{:S(2)}) collective-permute-start(bf16[384,256]{1,0:T(8,128)(2,1)S(1)} %multiply_convert_fusion.1), channel_id=1, source_target_pairs={{0,16},{3,18},{4,20},{7,22},{8,24},{11,26},{12,28},{15,30},{16,1},... | collective-permute-start | bytes 589832 | tf_op jit(solution)/shard_map/ppermute | solution.py:18
  55.0 6.0 %collective-permute-done.24 = bf16[384,256]{1,0:T(8,128)(2,1)S(1)} collective-permute-done((bf16[384,256]{1,0:T(8,128)(2,1)S(1)}, bf16[384,256]{1,0:T(8,128)(2,1)S(1)}, u32[]{:S(2)}, u32[]{:S(2)}) %collective-permute-start.24) | collective-permute-done | bytes 196640 | tf_op jit(solution)/shard_map/ppermute | solution.py:18
  64.3 1.6 %collective-permute-start.32 = (bf16[384,256]{1,0:T(8,128)(2,1)S(1)}, bf16[384,256]{1,0:T(8,128)(2,1)S(1)}, u32[]{:S(2)}, u32[]{:S(2)}) collective-permute-start(bf16[384,256]{1,0:T(8,128)(2,1)S(1)} %get-tuple-element.51.refs_0_), channel_id=1, source_target_pairs={{0,8},{1,9},{2,6},{3,7},{4,12},{5,13},{6,2},{7,3},{8,0},{9,1},{10,... | collective-permute-start | bytes 589832 | tf_op jit(solution)/shard_map/ppermute | solution.py:18
  66.0 2.3 %shard_map.107 = (f32[128,128]{1,0:T(8,128)S(1)}, f32[128,128]{1,0:T(8,128)S(1)}) custom-call(s32[256]{0:T(256)S(1)} %select_reduce_fusion.code_ref, s32[5]{0:T(128)S(1)} %convert_reduce_fusion.1.ends_ref, bf16[768,256]{1,0:T(8,128)(2,1)S(1)} %pad_maximum_fusion.emb_ref, bf16[384,256]{1,0:T(8,128)(2,1)S(1)} %get-tuple-element.51.refs_0_, ...), custom_call_target="tpu_custom_call" | custom-call | tf_op jit(solution)/shard_map/pallas_call | solution.py:188
  68.5 1.4 %collective-permute-start.31 = (bf16[384,256]{1,0:T(8,128)(2,1)S(1)}, bf16[384,256]{1,0:T(8,128)(2,1)S(1)}, u32[]{:S(2)}, u32[]{:S(2)}) collective-permute-start(bf16[384,256]{1,0:T(8,128)(2,1)S(1)} %collective-permute-done.25.refs_1_), channel_id=1, source_target_pairs={{0,2},{1,3},{2,0},{3,1},{4,6},{5,7},{6,4},{7,5},{8,10},{9,11},{10,... | collective-permute-start | bytes 589832 | tf_op jit(solution)/shard_map/ppermute | solution.py:18
  69.9 2.7 %collective-permute-done.21.refs_0_ = bf16[384,256]{1,0:T(8,128)(2,1)S(1)} collective-permute-done((bf16[384,256]{1,0:T(8,128)(2,1)S(1)}, bf16[384,256]{1,0:T(8,128)(2,1)S(1)}, u32[]{:S(2)}, u32[]{:S(2)}) %collective-permute-start.21) | collective-permute-done | bytes 196640 | tf_op jit(solution)/shard_map/ppermute | solution.py:18
  75.0 3.8 %shard_map.108 = (f32[128,128]{1,0:T(8,128)S(1)}, f32[128,128]{1,0:T(8,128)S(1)}) custom-call(s32[256]{0:T(256)S(1)} %select_reduce_fusion.code_ref, s32[5]{0:T(128)S(1)} %convert_reduce_fusion.1.ends_ref, bf16[768,256]{1,0:T(8,128)(2,1)S(1)} %pad_maximum_fusion.emb_ref, bf16[384,256]{1,0:T(8,128)(2,1)S(1)} %collective-permute-done.21.refs_0_, ...), custom_call_target="tpu_custom_call" | custom-call | tf_op jit(solution)/shard_map/pallas_call | solution.py:188
  80.5 1.4 %collective-permute-start.23 = (bf16[384,256]{1,0:T(8,128)(2,1)S(1)}, bf16[384,256]{1,0:T(8,128)(2,1)S(1)}, u32[]{:S(2)}, u32[]{:S(2)}) collective-permute-start(bf16[384,256]{1,0:T(8,128)(2,1)S(1)} %collective-permute-done.22.refs_0_), channel_id=1, source_target_pairs={{0,2},{1,3},{2,0},{3,1},{4,6},{5,7},{6,4},{7,5},{8,10},{9,11},{10,... | collective-permute-start | bytes 589832 | tf_op jit(solution)/shard_map/ppermute | solution.py:18
  82.5 1.6 %shard_map.109 = (f32[128,128]{1,0:T(8,128)S(1)}, f32[128,128]{1,0:T(8,128)S(1)}) custom-call(s32[256]{0:T(256)S(1)} %select_reduce_fusion.code_ref, s32[5]{0:T(128)S(1)} %convert_reduce_fusion.1.ends_ref, bf16[768,256]{1,0:T(8,128)(2,1)S(1)} %pad_maximum_fusion.emb_ref, bf16[384,256]{1,0:T(8,128)(2,1)S(1)} %collective-permute-done.22.refs_0_, ...), custom_call_target="tpu_custom_call" | custom-call | tf_op jit(solution)/shard_map/pallas_call | solution.py:188
  84.2 2.2 %shard_map.110 = (f32[128,128]{1,0:T(8,128)}, f32[128,128]{1,0:T(8,128)}) custom-call(s32[256]{0:T(256)S(1)} %select_reduce_fusion.code_ref, s32[5]{0:T(128)S(1)} %convert_reduce_fusion.1.ends_ref, bf16[768,256]{1,0:T(8,128)(2,1)S(1)} %pad_maximum_fusion.emb_ref, bf16[384,256]{1,0:T(8,128)(2,1)S(1)} %collective-permute-done.23.refs_0_, ...), custom_call_target="tpu_custom_call" | custom-call | tf_op jit(solution)/shard_map/pallas_call | solution.py:188
  (93 shorter events, 23.8 us)
Async XLA Ops:
  1.7 9.7 %collective-permute-start.4 = (bf16[384,256]{1,0:T(8,128)(2,1)S(1)}, bf16[384,256]{1,0:T(8,128)(2,1)S(1)}, u32[]{:S(2)}, u32[]{:S(2)}) collective-permute-start(bf16[384,256]{1,0:T(8,128)(2,1)S(1)} %slice.22), channel_id=1, source_target_pairs={{0,16},{3,18},{4,20},{7,22},{8,24},{11,26},{12,28},{15,30},{16,1},... | collective-permute-start | bytes 589832 | tf_op jit(solution)/shard_map/ppermute | solution.py:18
  12.5 9.8 %collective-permute-start = (bf16[384,256]{1,0:T(8,128)(2,1)S(1)}, bf16[384,256]{1,0:T(8,128)(2,1)S(1)}, u32[]{:S(2)}, u32[]{:S(2)}) collective-permute-start(bf16[384,256]{1,0:T(8,128)(2,1)S(1)} %get-tuple-element.58), channel_id=1, source_target_pairs={{0,16},{3,18},{4,20},{7,22},{8,24},{11,26},{12,28},{15,30},{16,1},... | collective-permute-start | bytes 589832 | tf_op jit(solution)/shard_map/ppermute | solution.py:18
  15.4 10.2 %collective-permute-start.8 = (bf16[384,256]{1,0:T(8,128)(2,1)S(1)}, bf16[384,256]{1,0:T(8,128)(2,1)S(1)}, u32[]{:S(2)}, u32[]{:S(2)}) collective-permute-start(bf16[384,256]{1,0:T(8,128)(2,1)S(1)} %get-tuple-element.57.refs_1_), channel_id=1, source_target_pairs={{0,2},{1,3},{2,0},{3,1},{4,6},{5,7},{6,4},{7,5},{8,10},{9,11},{10,... | collective-permute-start | bytes 589832 | tf_op jit(solution)/shard_map/ppermute | solution.py:18
  16.4 11.2 %collective-permute-start.5 = (bf16[384,256]{1,0:T(8,128)(2,1)S(1)}, bf16[384,256]{1,0:T(8,128)(2,1)S(1)}, u32[]{:S(2)}, u32[]{:S(2)}) collective-permute-start(bf16[384,256]{1,0:T(8,128)(2,1)S(1)} %get-tuple-element.57.refs_1_), channel_id=1, source_target_pairs={{0,4},{1,5},{2,10},{3,11},{4,0},{5,1},{6,14},{7,15},{8,12},{9,13},... | collective-permute-start | bytes 589832 | tf_op jit(solution)/shard_map/ppermute | solution.py:18
  18.7 8.9 %collective-permute-start.6 = (bf16[384,256]{1,0:T(8,128)(2,1)S(1)}, bf16[384,256]{1,0:T(8,128)(2,1)S(1)}, u32[]{:S(2)}, u32[]{:S(2)}) collective-permute-start(bf16[384,256]{1,0:T(8,128)(2,1)S(1)} %get-tuple-element.57.refs_1_), channel_id=1, source_target_pairs={{0,8},{1,9},{2,6},{3,7},{4,12},{5,13},{6,2},{7,3},{8,0},{9,1},{10,... | collective-permute-start | bytes 589832 | tf_op jit(solution)/shard_map/ppermute | solution.py:18
  25.6 6.3 %collective-permute-start.1 = (bf16[384,256]{1,0:T(8,128)(2,1)S(1)}, bf16[384,256]{1,0:T(8,128)(2,1)S(1)}, u32[]{:S(2)}, u32[]{:S(2)}) collective-permute-start(bf16[384,256]{1,0:T(8,128)(2,1)S(1)} %broadcast_select_fusion.3.refs_0_), channel_id=1, source_target_pairs={{0,4},{1,5},{2,10},{3,11},{4,0},{5,1},{6,14},{7,15},{8,12},{9,13},... | collective-permute-start | bytes 589832 | tf_op jit(solution)/shard_map/ppermute | solution.py:18
  25.6 7.8 %collective-permute-start.12 = (bf16[384,256]{1,0:T(8,128)(2,1)S(1)}, bf16[384,256]{1,0:T(8,128)(2,1)S(1)}, u32[]{:S(2)}, u32[]{:S(2)}) collective-permute-start(bf16[384,256]{1,0:T(8,128)(2,1)S(1)} %broadcast_select_fusion.3.refs_0_), channel_id=1, source_target_pairs={{0,8},{1,9},{2,6},{3,7},{4,12},{5,13},{6,2},{7,3},{8,0},{9,1},{10,... | collective-permute-start | bytes 589832 | tf_op jit(solution)/shard_map/ppermute | solution.py:18
  27.6 7.1 %collective-permute-start.11 = (bf16[384,256]{1,0:T(8,128)(2,1)S(1)}, bf16[384,256]{1,0:T(8,128)(2,1)S(1)}, u32[]{:S(2)}, u32[]{:S(2)}) collective-permute-start(bf16[384,256]{1,0:T(8,128)(2,1)S(1)} %collective-permute-done.5.refs_1_), channel_id=1, source_target_pairs={{0,2},{1,3},{2,0},{3,1},{4,6},{5,7},{6,4},{7,5},{8,10},{9,11},{10,... | collective-permute-start | bytes 589832 | tf_op jit(solution)/shard_map/ppermute | solution.py:18
  28.0 8.8 %collective-permute-start.9 = (bf16[384,256]{1,0:T(8,128)(2,1)S(1)}, bf16[384,256]{1,0:T(8,128)(2,1)S(1)}, u32[]{:S(2)}, u32[]{:S(2)}) collective-permute-start(bf16[384,256]{1,0:T(8,128)(2,1)S(1)} %collective-permute-done.5.refs_1_), channel_id=1, source_target_pairs={{0,8},{1,9},{2,6},{3,7},{4,12},{5,13},{6,2},{7,3},{8,0},{9,1},{10,... | collective-permute-start | bytes 589832 | tf_op jit(solution)/shard_map/ppermute | solution.py:18
  29.0 6.0 %collective-permute-start.14 = (bf16[384,256]{1,0:T(8,128)(2,1)S(1)}, bf16[384,256]{1,0:T(8,128)(2,1)S(1)}, u32[]{:S(2)}, u32[]{:S(2)}) collective-permute-start(bf16[384,256]{1,0:T(8,128)(2,1)S(1)} %collective-permute-done.6.refs_5_), channel_id=1, source_target_pairs={{0,2},{1,3},{2,0},{3,1},{4,6},{5,7},{6,4},{7,5},{8,10},{9,11},{10,... | collective-permute-start | bytes 589832 | tf_op jit(solution)/shard_map/ppermute | solution.py:18
  33.4 5.5 %collective-permute-start.2 = (bf16[384,256]{1,0:T(8,128)(2,1)S(1)}, bf16[384,256]{1,0:T(8,128)(2,1)S(1)}, u32[]{:S(2)}, u32[]{:S(2)}) collective-permute-start(bf16[384,256]{1,0:T(8,128)(2,1)S(1)} %collective-permute-done.1.refs_0_), channel_id=1, source_target_pairs={{0,8},{1,9},{2,6},{3,7},{4,12},{5,13},{6,2},{7,3},{8,0},{9,1},{10,... | collective-permute-start | bytes 589832 | tf_op jit(solution)/shard_map/ppermute | solution.py:18
  41.0 6.4 %collective-permute-start.18 = (bf16[384,256]{1,0:T(8,128)(2,1)S(1)}, bf16[384,256]{1,0:T(8,128)(2,1)S(1)}, u32[]{:S(2)}, u32[]{:S(2)}) collective-permute-start(bf16[384,256]{1,0:T(8,128)(2,1)S(1)} %get-tuple-element.55), channel_id=1, source_target_pairs={{1,0},{2,3},{5,4},{6,7},{9,8},{10,11},{13,12},{14,15},{17,16},{18,... | collective-permute-start | bytes 589832 | tf_op jit(solution)/shard_map/ppermute | solution.py:18
  42.5 8.8 %collective-permute-start.16 = (bf16[384,256]{1,0:T(8,128)(2,1)S(1)}, bf16[384,256]{1,0:T(8,128)(2,1)S(1)}, u32[]{:S(2)}, u32[]{:S(2)}) collective-permute-start(bf16[384,256]{1,0:T(8,128)(2,1)S(1)} %get-tuple-element.56), channel_id=1, source_target_pairs={{1,0},{2,3},{5,4},{6,7},{9,8},{10,11},{13,12},{14,15},{17,16},{18,... | collective-permute-start | bytes 589832 | tf_op jit(solution)/shard_map/ppermute | solution.py:18
  47.9 7.1 %collective-permute-start.19 = (bf16[384,256]{1,0:T(8,128)(2,1)S(1)}, bf16[384,256]{1,0:T(8,128)(2,1)S(1)}, u32[]{:S(2)}, u32[]{:S(2)}) collective-permute-start(bf16[384,256]{1,0:T(8,128)(2,1)S(1)} %multiply_convert_fusion), channel_id=1, source_target_pairs={{0,1},{3,2},{4,5},{7,6},{8,9},{11,10},{12,13},{15,14},{16,17},{19,... | collective-permute-start | bytes 589832 | tf_op jit(solution)/shard_map/ppermute | solution.py:18
  49.4 11.7 %collective-permute-start.24 = (bf16[384,256]{1,0:T(8,128)(2,1)S(1)}, bf16[384,256]{1,0:T(8,128)(2,1)S(1)}, u32[]{:S(2)}, u32[]{:S(2)}) collective-permute-start(bf16[384,256]{1,0:T(8,128)(2,1)S(1)} %multiply_convert_fusion), channel_id=1, source_target_pairs={{0,16},{3,18},{4,20},{7,22},{8,24},{11,26},{12,28},{15,30},{16,1},... | collective-permute-start | bytes 589832 | tf_op jit(solution)/shard_map/ppermute | solution.py:18
  51.8 10.2 %collective-permute-start.17 = (bf16[384,256]{1,0:T(8,128)(2,1)S(1)}, bf16[384,256]{1,0:T(8,128)(2,1)S(1)}, u32[]{:S(2)}, u32[]{:S(2)}) collective-permute-start(bf16[384,256]{1,0:T(8,128)(2,1)S(1)} %multiply_convert_fusion.1), channel_id=1, source_target_pairs={{0,1},{3,2},{4,5},{7,6},{8,9},{11,10},{12,13},{15,14},{16,17},{19,... | collective-permute-start | bytes 589832 | tf_op jit(solution)/shard_map/ppermute | solution.py:18
  53.1 10.1 %collective-permute-start.20 = (bf16[384,256]{1,0:T(8,128)(2,1)S(1)}, bf16[384,256]{1,0:T(8,128)(2,1)S(1)}, u32[]{:S(2)}, u32[]{:S(2)}) collective-permute-start(bf16[384,256]{1,0:T(8,128)(2,1)S(1)} %multiply_convert_fusion.1), channel_id=1, source_target_pairs={{0,16},{3,18},{4,20},{7,22},{8,24},{11,26},{12,28},{15,30},{16,1},... | collective-permute-start | bytes 589832 | tf_op jit(solution)/shard_map/ppermute | solution.py:18
  62.0 6.4 %collective-permute-start.25 = (bf16[384,256]{1,0:T(8,128)(2,1)S(1)}, bf16[384,256]{1,0:T(8,128)(2,1)S(1)}, u32[]{:S(2)}, u32[]{:S(2)}) collective-permute-start(bf16[384,256]{1,0:T(8,128)(2,1)S(1)} %get-tuple-element.49.refs_1_), channel_id=1, source_target_pairs={{0,4},{1,5},{2,10},{3,11},{4,0},{5,1},{6,14},{7,15},{8,12},{9,13},... | collective-permute-start | bytes 589832 | tf_op jit(solution)/shard_map/ppermute | solution.py:18
  62.0 6.5 %collective-permute-start.26 = (bf16[384,256]{1,0:T(8,128)(2,1)S(1)}, bf16[384,256]{1,0:T(8,128)(2,1)S(1)}, u32[]{:S(2)}, u32[]{:S(2)}) collective-permute-start(bf16[384,256]{1,0:T(8,128)(2,1)S(1)} %get-tuple-element.49.refs_1_), channel_id=1, source_target_pairs={{0,8},{1,9},{2,6},{3,7},{4,12},{5,13},{6,2},{7,3},{8,0},{9,1},{10,... | collective-permute-start | bytes 589832 | tf_op jit(solution)/shard_map/ppermute | solution.py:18
  64.2 8.3 %collective-permute-start.21 = (bf16[384,256]{1,0:T(8,128)(2,1)S(1)}, bf16[384,256]{1,0:T(8,128)(2,1)S(1)}, u32[]{:S(2)}, u32[]{:S(2)}) collective-permute-start(bf16[384,256]{1,0:T(8,128)(2,1)S(1)} %get-tuple-element.51.refs_0_), channel_id=1, source_target_pairs={{0,4},{1,5},{2,10},{3,11},{4,0},{5,1},{6,14},{7,15},{8,12},{9,13},... | collective-permute-start | bytes 589832 | tf_op jit(solution)/shard_map/ppermute | solution.py:18
  64.3 9.2 %collective-permute-start.32 = (bf16[384,256]{1,0:T(8,128)(2,1)S(1)}, bf16[384,256]{1,0:T(8,128)(2,1)S(1)}, u32[]{:S(2)}, u32[]{:S(2)}) collective-permute-start(bf16[384,256]{1,0:T(8,128)(2,1)S(1)} %get-tuple-element.51.refs_0_), channel_id=1, source_target_pairs={{0,8},{1,9},{2,6},{3,7},{4,12},{5,13},{6,2},{7,3},{8,0},{9,1},{10,... | collective-permute-start | bytes 589832 | tf_op jit(solution)/shard_map/ppermute | solution.py:18
  73.6 5.3 %collective-permute-start.29 = (bf16[384,256]{1,0:T(8,128)(2,1)S(1)}, bf16[384,256]{1,0:T(8,128)(2,1)S(1)}, u32[]{:S(2)}, u32[]{:S(2)}) collective-permute-start(bf16[384,256]{1,0:T(8,128)(2,1)S(1)} %collective-permute-done.25.refs_1_), channel_id=1, source_target_pairs={{0,8},{1,9},{2,6},{3,7},{4,12},{5,13},{6,2},{7,3},{8,0},{9,1},{10,... | collective-permute-start | bytes 589832 | tf_op jit(solution)/shard_map/ppermute | solution.py:18
  73.7 6.8 %collective-permute-start.22 = (bf16[384,256]{1,0:T(8,128)(2,1)S(1)}, bf16[384,256]{1,0:T(8,128)(2,1)S(1)}, u32[]{:S(2)}, u32[]{:S(2)}) collective-permute-start(bf16[384,256]{1,0:T(8,128)(2,1)S(1)} %collective-permute-done.21.refs_0_), channel_id=1, source_target_pairs={{0,8},{1,9},{2,6},{3,7},{4,12},{5,13},{6,2},{7,3},{8,0},{9,1},{10,... | collective-permute-start | bytes 589832 | tf_op jit(solution)/shard_map/ppermute | solution.py:18
  78.9 5.3 %collective-permute-start.35 = (bf16[384,256]{1,0:T(8,128)(2,1)S(1)}, bf16[384,256]{1,0:T(8,128)(2,1)S(1)}, u32[]{:S(2)}, u32[]{:S(2)}) collective-permute-start(bf16[384,256]{1,0:T(8,128)(2,1)S(1)} %collective-permute-done.29.refs_1_), channel_id=1, source_target_pairs={{0,2},{1,3},{2,0},{3,1},{4,6},{5,7},{6,4},{7,5},{8,10},{9,11},{10,... | collective-permute-start | bytes 589832 | tf_op jit(solution)/shard_map/ppermute | solution.py:18
  (19 other events, 169.8 us)

commit v2 on v1

--- a/solution.py
+++ b/solution.py
@@ -20,9 +20,29 @@
     )
 
 
-def aggregate_kernel(rows_of, members, fetch, sections, has_tiles, has_previous, live_ref, *refs):
-    n_pieces = sum(len(rows) for rows in rows_of)
-    piece_refs, refs = refs[:n_pieces], refs[n_pieces:]
+def plan(blocks):
+    arrays, places = [], []
+    for block in blocks:
+        places.append([])
+        for array, start, to, rows in block:
+            at = [i for i, known in enumerate(arrays) if known is array]
+            if not at:
+                arrays.append(array)
+                at = [len(arrays) - 1]
+            places[-1].append((at[0], start, to, rows))
+    return arrays, places
+
+
+def whole(parts):
+    pieces, to = [], 0
+    for part in parts:
+        pieces.append((part, 0, to, part.shape[0]))
+        to += part.shape[0]
+    return pieces
+
+
+def aggregate_kernel(n_arrays, places, members, fetch, sections, has_tiles, has_previous, live_ref, *refs):
+    source_refs, refs = refs[:n_arrays], refs[n_arrays:]
     previous_ref, refs = (refs[0], refs[1:]) if has_previous else (None, refs)
     if has_tiles:
         tile_refs, (out_ref,) = refs[: len(members)], refs[len(members) :]
@@ -36,7 +56,7 @@
     def section(slot):
         return member ^ jnp.where(odd > 0, slot[1], slot[0])
 
-    places = [section(slot) for slot in members]
+    sections_of = [section(slot) for slot in members]
     blocksize = out_ref.shape[0]
     copies = []
     if not has_tiles:
@@ -51,19 +71,16 @@
         out_ref[...] = previous_ref[...]
     else:
         out_ref[...] = jnp.zeros_like(out_ref)
-    at = 0
-    for b, rows in enumerate(rows_of):
-        pieces = piece_refs[at : at + len(rows)]
-        at += len(rows)
-
-        @pl.when(live_ref[0, places[b]] > 0)
+    for b, pieces in enumerate(places):
+
+        @pl.when(live_ref[0, sections_of[b]] > 0)
         def _():
             if not has_tiles:
                 copies[b].wait()
-            for piece, to in zip(pieces, rows):
+            for i, start, to, rows in pieces:
                 out_ref[...] += jnp.dot(
-                    tile_refs[b][:, to : to + piece.shape[0]],
-                    piece[...],
+                    tile_refs[b][:, to : to + rows],
+                    source_refs[i][start : start + rows, :],
                     preferred_element_type=jnp.float32,
                 )
 
@@ -79,8 +96,7 @@
     blocksize = adjacency.shape[0]
     channels = blocks[0][0][0].shape[1]
     fetch = list(fetch)
-    pieces = [piece for block in blocks for piece, _ in block]
-    rows_of = [[to for _, to in block] for block in blocks]
+    arrays, places = plan(blocks)
     extra = [] if previous is None else [previous]
     extra_tiles = [] if tiles is None else list(tiles)
     tile = jax.ShapeDtypeStruct((blocksize, blocksize), adjacency.dtype)
@@ -88,7 +104,8 @@
     out = pl.pallas_call(
         functools.partial(
             aggregate_kernel,
-            rows_of,
+            len(arrays),
+            places,
             members,
             fetch,
             adjacency.shape[1] // blocksize,
@@ -96,7 +113,7 @@
             previous is not None,
         ),
         in_specs=[pl.BlockSpec(memory_space=pltpu.SMEM)]
-        + vmem(len(pieces) + len(extra) + len(extra_tiles))
+        + vmem(len(arrays) + len(extra) + len(extra_tiles))
         + ([pl.BlockSpec(memory_space=pl.ANY)] if tiles is None else []),
         out_specs=vmem(1 + len(fetch)),
         out_shape=[jax.ShapeDtypeStruct((blocksize, channels), jnp.float32)] + [tile] * len(fetch),
@@ -109,13 +126,12 @@
         compiler_params=pltpu.CompilerParams(
             vmem_limit_bytes=(44 if tiles is None else 8) * 1024 * 1024
         ),
-    )(tile_live, *pieces, *extra, *(extra_tiles if tiles is not None else [adjacency]))
+    )(tile_live, *arrays, *extra, *(extra_tiles if tiles is not None else [adjacency]))
     return out[0], out[1:]
 
 
-def score_kernel(rows_of, which, has_previous, code_ref, ends_ref, emb_ref, *refs):
-    n_pieces = sum(len(rows) for rows in rows_of)
-    piece_refs, refs = refs[:n_pieces], refs[n_pieces:]
+def score_kernel(n_arrays, places, which, has_previous, code_ref, ends_ref, emb_ref, *refs):
+    key_refs, refs = refs[:n_arrays], refs[n_arrays:]
     previous_refs, refs = (refs[:2], refs[2:]) if has_previous else (None, refs)
     pos_ref, neg_ref, scores, losses = refs
     blocksize, channels = emb_ref.shape
@@ -126,23 +142,21 @@
         losses[n_pairs:, :] = previous_refs[1][...]
     else:
         losses[...] = jnp.zeros_like(losses)
-    scores[:, len(rows_of) * blocksize :, :] = jnp.zeros((n_tiles, EDGE, PAIR_ROWS), jnp.float32)
-    at = 0
-    for b, rows in enumerate(rows_of):
-        for piece, to in zip(piece_refs[at : at + len(rows)], rows):
+    scores[:, len(places) * blocksize :, :] = jnp.zeros((n_tiles, EDGE, PAIR_ROWS), jnp.float32)
+    for b, pieces in enumerate(places):
+        for i, start, to, rows in pieces:
             first = b * blocksize + to
             for t in range(0, n_tiles, WIDE // PAIR_ROWS):
                 product = lax.dot_general(
-                    piece[...],
+                    key_refs[i][start : start + rows, :],
                     emb_ref[t * PAIR_ROWS : t * PAIR_ROWS + WIDE, :],
                     (((1,), (1,)), ((), ())),
                     preferred_element_type=jnp.float32,
                 )
                 for u in range(WIDE // PAIR_ROWS):
-                    scores[t + u, first : first + piece.shape[0], :] = product[
+                    scores[t + u, first : first + rows, :] = product[
                         :, u * PAIR_ROWS : (u + 1) * PAIR_ROWS
                     ]
-        at += len(rows)
 
     row_of = lax.broadcasted_iota(jnp.int32, (EDGE, PAIR_ROWS), 0)
     scale = math.log2(math.e) / math.sqrt(channels)
@@ -182,12 +196,11 @@
     blocksize, channels = embedding_block.shape
     n_rows = len(blocks) * blocksize
     loss = jax.ShapeDtypeStruct((n_pairs, PAIR_ROWS), jnp.float32)
-    pieces = [piece for block in blocks for piece, _ in block]
-    rows_of = [[to for _, to in block] for block in blocks]
+    arrays, places = plan(blocks)
     extra = [] if previous is None else list(previous)
     return pl.pallas_call(
-        functools.partial(score_kernel, rows_of, which, previous is not None),
-        in_specs=[pl.BlockSpec(memory_space=pltpu.SMEM)] * 2 + vmem(1 + len(pieces) + len(extra)),
+        functools.partial(score_kernel, len(arrays), places, which, previous is not None),
+        in_specs=[pl.BlockSpec(memory_space=pltpu.SMEM)] * 2 + vmem(1 + len(arrays) + len(extra)),
         out_specs=vmem(2),
         scratch_shapes=[
             pltpu.VMEM((blocksize // PAIR_ROWS, n_rows + EDGE, PAIR_ROWS), jnp.float32),
@@ -195,7 +208,7 @@
         ],
         out_shape=[loss, loss],
         compiler_params=pltpu.CompilerParams(vmem_limit_bytes=24 * 1024 * 1024),
-    )(codes, ends, embedding_block, *pieces, *extra)
+    )(codes, ends, embedding_block, *arrays, *extra)
 
 
 def order_pairs(pairs, member, sets, blocksize):
@@ -229,11 +242,8 @@
         self.halved = n_rep == 2 and self.groups == 2 and sections == 8
         if self.halved:
             self.slots = [(0, 0), (1, 1), (2, 4), (5, 3), (4, 2), (3, 5), (6, 6), (7, 7)]
-            self.sets = [[0, 1], [2, 3, 4, 5], [6], [7]]
         else:
             self.slots = [(j, j) for j in range(sections)]
-            self.sets = [list(range(sections))]
-        self.members = [[self.slots[slot] for slot in members] for members in self.sets]
 
     def flip(self, block, stride):
         return permute(
@@ -247,49 +257,34 @@
             self.n_rep,
         )
 
-    def to_holder(self, block):
-        return permute(
-            block, [((r, p), (r, r & 1)) for r, p in self.everyone if p != r & 1], self.n_rep
-        )
-
-    def from_holder(self, block):
-        return permute(
-            block, [((r, p), (r, 1 - p)) for r, p in self.everyone if p == r & 1], self.n_rep
-        )
-
-    def run_halved(self, held, own, consume):
+    def swap(self, block):
+        return permute(block, [((r, p), (r, 1 - p)) for r, p in self.everyone], self.n_rep)
+
+    def run_halved(self, parts, consume):
         n = self.sections
-        half = own[0].shape[0]
         across = [
             ((r, p), ((r + n) % self.n_row, r // n)) for r, p in self.everyone if p == r & 1
         ]
-        start, near, first, second = [], [], [], []
-        came = [permute(part, across, self.n_rep) for part in held]
-        for own_part, came_part in zip(own, came):
-            part = jnp.where(self.group == self.rep, own_part, came_part)
-            start.append(part)
-            first.append(self.flip_either(part, 2, 4))
-            second.append(self.flip_either(part, 4, 2))
-            near.append(self.flip(part, 1))
-
-        def whole(parts):
-            return [(part, i * half) for i, part in enumerate(parts)]
-
-        def near_of(parts):
-            return [self.flip(part, 1) for part in parts]
-
-        done = consume(0, [whole(start), whole(near)], None)
-        first[1], second[1], done = lax.optimization_barrier((first[1], second[1], done))
-        third = [self.flip_either(part, 4, 2) for part in first]
-        done = consume(
-            1,
-            [whole(x) for parts in (first, second) for x in (parts, near_of(parts))],
-            done,
-        )
+        came = [permute(part, across, self.n_rep) for part in parts]
+        start = [jnp.where(self.group == self.rep, x, y) for x, y in zip(parts, came)]
+        first = [self.flip_either(part, 2, 4) for part in start]
+        second = [self.flip_either(part, 4, 2) for part in start]
+        near = [self.flip(part, 1) for part in start]
+        done = consume([whole(start), whole(near)], None)
+        halves = first
+        if len(first) == 1:
+            half = first[0].shape[0] // 2
+            halves = [first[0][:half], first[0][half:]]
+        third = [self.flip_either(part, 4, 2) for part in halves]
+        near_first = [self.flip(part, 1) for part in first]
+        near_second = [self.flip(part, 1) for part in second]
+        done = consume([whole(x) for x in (first, near_first, second, near_second)], done)
         third[1], done = lax.optimization_barrier((third[1], done))
-        near_third = near_of(third)
-        done = consume(2, [whole(third)], done)
-        return consume(3, [whole(near_third)], done)
+        if len(first) == 1:
+            third[0], done = lax.optimization_barrier((third[0], done))
+        near_third = [self.flip(part, 1) for part in third]
+        done = consume([whole(third)], done)
+        return consume([whole(near_third)], done)
 
     def run_whole(self, block, consume):
         start = block
@@ -308,7 +303,7 @@
         for b in reversed(range(self.sections.bit_length() - 1)):
             for j in list(blocks):
                 blocks[j ^ (1 << b)] = self.flip(blocks[j], 1 << b)
-        return consume(0, [[(blocks[j], 0)] for j in range(self.sections)], None)
+        return consume([whole([blocks[j]]) for j in range(self.sections)], None)
 
 
 def per_device(
@@ -319,24 +314,26 @@
     n_pairs = pos_pairs.shape[1]
     share = blocksize // n_rep
     spread = Spread(n_row, n_rep, sections)
-    rep, sets = spread.rep, spread.members
-
-    fetched = {}
-
-    def add_tiles(which, blocks, earlier):
-        members = sets[which]
-        last = [slot for later in sets[2:] for slot in later] if which == 1 else []
+    rep, slots = spread.rep, spread.slots
+
+    fetched, added = {}, []
+
+    def add_tiles(blocks, earlier):
+        members = slots[len(added) : len(added) + len(blocks)]
+        added.extend(members)
+        left = slots[len(added) :]
+        last = left if 0 < len(left) <= 2 and not fetched else []
         tiles = [fetched[slot] for slot in members] if members[0] in fetched else None
         total, more = aggregate(tile_live, adjacency, blocks, members, earlier, tiles, last)
         fetched.update(zip(last, more))
         return total
 
     if spread.halved:
-        parts = [features[:share], features[share:]]
-        partial = spread.run_halved(parts, parts, add_tiles)
+        partial = spread.run_halved([features], add_tiles)
     else:
         partial = spread.run_whole(features, add_tiles)
 
+    sets = [slots[:2], slots[2:6], [slots[6]], [slots[7]]] if spread.halved else [slots]
     codes, ends = order_pairs(
         jnp.concatenate([pos_pairs[0], neg_pairs[0]], axis=0), spread.member, sets, blocksize
     )
@@ -349,24 +346,30 @@
         return (projected * scale).astype(jnp.bfloat16)
 
     if spread.halved:
-        held = []
-        for i, feats in enumerate(parts):
-            mine = partial[i * share : (i + 1) * share]
-            other = spread.to_holder(mine.astype(jnp.bfloat16))
-            held.append(embed(feats, mine + other.astype(jnp.float32)))
+        own = []
+        for i in range(2):
+            rows = slice(i * share, (i + 1) * share)
+            other = spread.swap(partial[rows].astype(jnp.bfloat16))
+            own.append(embed(features[rows], partial[rows] + other.astype(jnp.float32)))
     else:
         own_feats = lax.dynamic_slice_in_dim(features, rep * share, share, 0)
         embedding = embed(own_feats, lax.psum_scatter(partial, "rep", scatter_dimension=0, tiled=True))
 
-    def score(queries, which, blocks, earlier):
-        return score_pairs(codes, ends, which, queries, blocks, n_pairs, earlier)
+    scored, output = [], []
+
+    def score(queries, blocks, earlier):
+        if len(scored) == 1:
+            own_now, earlier = lax.optimization_barrier((own, earlier))
+            rows = jnp.where(rep == 0, own_now[0], own_now[1])
+            rows, earlier = lax.optimization_barrier((rows, earlier))
+            output.append(rows)
+        scored.append(len(blocks))
+        return score_pairs(codes, ends, len(scored) - 1, queries, blocks, n_pairs, earlier)
 
     if spread.halved:
-        holder = rep == spread.member & 1
-        own = [jnp.where(holder, part, spread.from_holder(part)) for part in held]
         block = jnp.concatenate(own, axis=0)
-        embedding = jnp.where(rep == 0, own[0], own[1])
-        losses = spread.run_halved(held, own, functools.partial(score, block))
+        losses = spread.run_halved(own, functools.partial(score, block))
+        embedding = output[0]
     else:
         block = lax.all_gather(embedding, "rep", axis=0, tiled=True)
         losses = spread.run_whole(block, functools.partial(score, block))

time: 86.9 us -> 83.1 us (0.956)
  waiting for transfers between devices: 23.6 us -> 20.6 us
  Pallas kernels: 12.4 us -> 14.3 us
  other arithmetic: 2.75 us -> 1.72 us
  starting transfers between devices: 44.4 us -> 43.4 us
    ppermute x36 -> x28, waiting for transfers between devices: 23.6 us -> 20.6 us  [permute(): lax.ppermute(block, ('row', 'rep'), [(a[0] * n_rep + a[1], b[0] * n_rep +...]
    pallas_call x8, Pallas kernels: 12.4 us -> 14.3 us  [the longest x4 10 us: score_pairs(): pl.pallas_call(functools.partial(score_kernel, len(arrays), places, which...]
    select_n x5 -> x4, other arithmetic: 2.03 us -> 0.99 us  [the longest x1 0.7 us: score(): rows = jnp.where(rep == 0, own_now[0], own_now[1])]
    ppermute x36 -> x28, starting transfers between devices: 44.4 us -> 43.4 us  [permute(): lax.ppermute(block, ('row', 'rep'), [(a[0] * n_rep + a[1], b[0] * n_rep +...]
    slice x2, local copies, waits for them, and re-layouts: 1.06 us -> 0.07 us  [the longest x1 0.04 us: per_device(): own.append(embed(features[rows], partial[rows] + other.astype(jnp.float32)))]
  transfers between devices with their start and end apart: 36 -> 28, of which waited for: 12 -> 9; matrix products, arithmetic and copies ran while one was open for 3% -> 4% of each run, Pallas kernels for 11% -> 14%
where the time goes in v2:
time: 83.1 us; the launch traced here: 82.9 us
  starting transfers between devices  43.4 us (52%)
  waiting for transfers between devices  20.6 us (25%)
  Pallas kernels  14.3 us (17%)
  other arithmetic  1.72 us (2%)
  matrix products  1.06 us (1%)
  between operations  0.99 us (1%)
    ppermute x28, starting transfers between devices, permute(): lax.ppermute(block, ('row', 'rep'), [(a[0] * n_rep + a[1], b[0] * n_rep +...  43.4 us
    ppermute x28, waiting for transfers between devices, permute(): lax.ppermute(block, ('row', 'rep'), [(a[0] * n_rep + a[1], b[0] * n_rep +...  20.6 us
    pallas_call x4, Pallas kernels, score_pairs(): pl.pallas_call(functools.partial(score_kernel, len(arrays), places, which...  10 us
    pallas_call x4, Pallas kernels, aggregate(): pl.pallas_call(functools.partial(aggregate_kernel, len(arrays), places, m...  4.27 us
  transfers between devices with their start and end apart: 28, of which 9 were waited for; matrix products, arithmetic and copies ran while one was open for 4% of the time, Pallas kernels for 14%

profile of v2, /device:TPU:3, one launch (start us, length us, event | category | flops | bytes accessed | tf_op | source)
XLA Modules:
  0.0 82.9 jit_solution(9105286825321253388)
XLA Ops:
  0.7 4.3 %collective-permute-start = (bf16[768,256]{1,0:T(8,128)(2,1)}, bf16[768,256]{1,0:T(8,128)(2,1)S(1)}, u32[]{:S(2)}, u32[]{:S(2)}) collective-permute-start(bf16[768,256]{1,0:T(8,128)(2,1)} %param.8), channel_id=1, source_target_pairs={{0,16},{3,18},{4,20},{7,22},{8,24},{11,26},{12,28},{15,30},{16,1},... | collective-permute-start | bytes 1179656 | tf_op jit(solution)/shard_map/ppermute | solution.py:18
  5.7 9.2 %collective-permute-done = bf16[768,256]{1,0:T(8,128)(2,1)S(1)} collective-permute-done((bf16[768,256]{1,0:T(8,128)(2,1)}, bf16[768,256]{1,0:T(8,128)(2,1)S(1)}, u32[]{:S(2)}, u32[]{:S(2)}) %collective-permute-start) | collective-permute-done | bytes 393248 | tf_op jit(solution)/shard_map/ppermute | solution.py:18
  15.6 1.2 %collective-permute-start.5 = (bf16[768,256]{1,0:T(8,128)(2,1)S(1)}, bf16[768,256]{1,0:T(8,128)(2,1)S(1)}, u32[]{:S(2)}, u32[]{:S(2)}) collective-permute-start(bf16[768,256]{1,0:T(8,128)(2,1)S(1)} %broadcast_select_fusion.refs_0_), channel_id=1, source_target_pairs={{0,8},{1,9},{2,6},{3,7},{4,12},{5,13},{6,2},{7,3},{8,0},{9,1},{10,... | collective-permute-start | bytes 1179656 | tf_op jit(solution)/shard_map/ppermute | solution.py:18
  16.8 2.3 %collective-permute-start.7 = (bf16[768,256]{1,0:T(8,128)(2,1)S(1)}, bf16[768,256]{1,0:T(8,128)(2,1)S(1)}, u32[]{:S(2)}, u32[]{:S(2)}) collective-permute-start(bf16[768,256]{1,0:T(8,128)(2,1)S(1)} %broadcast_select_fusion.refs_0_), channel_id=1, source_target_pairs={{0,2},{1,3},{2,0},{3,1},{4,6},{5,7},{6,4},{7,5},{8,10},{9,11},{10,... | collective-permute-start | bytes 1179656 | tf_op jit(solution)/shard_map/ppermute | solution.py:18
  19.1 2.8 %collective-permute-done.1.refs_0_ = bf16[768,256]{1,0:T(8,128)(2,1)S(1)} collective-permute-done((bf16[768,256]{1,0:T(8,128)(2,1)S(1)}, bf16[768,256]{1,0:T(8,128)(2,1)S(1)}, u32[]{:S(2)}, u32[]{:S(2)}) %collective-permute-start.1) | collective-permute-done | bytes 393248 | tf_op jit(solution)/shard_map/ppermute | solution.py:18
  22.0 5.1 %collective-permute-start.4 = (bf16[768,256]{1,0:T(8,128)(2,1)S(1)}, bf16[768,256]{1,0:T(8,128)(2,1)S(1)}, u32[]{:S(2)}, u32[]{:S(2)}) collective-permute-start(bf16[768,256]{1,0:T(8,128)(2,1)S(1)} %collective-permute-done.1.refs_0_), channel_id=1, source_target_pairs={{0,2},{1,3},{2,0},{3,1},{4,6},{5,7},{6,4},{7,5},{8,10},{9,11},{10,... | collective-permute-start | bytes 1179656 | tf_op jit(solution)/shard_map/ppermute | solution.py:18
  27.1 1.3 %collective-permute-start.3 = (bf16[384,256]{1,0:T(8,128)(2,1)S(1)}, bf16[384,256]{1,0:T(8,128)(2,1)S(1)}, u32[]{:S(2)}, u32[]{:S(2)}) collective-permute-start(bf16[384,256]{1,0:T(8,128)(2,1)S(1)} %get-tuple-element.57), channel_id=1, source_target_pairs={{0,8},{1,9},{2,6},{3,7},{4,12},{5,13},{6,2},{7,3},{8,0},{9,1},{10,... | collective-permute-start | bytes 589832 | tf_op jit(solution)/shard_map/ppermute | solution.py:18
  29.7 1.9 %shard_map.104 = (f32[768,256]{1,0:T(8,128)S(1)}, bf16[768,768]{1,0:T(8,128)(2,1)S(1)}, bf16[768,768]{1,0:T(8,128)(2,1)S(1)}) custom-call(s32[1,8]{1,0:T(1,128)S(1)} %copy-done.1, bf16[768,256]{1,0:T(8,128)(2,1)S(1)} %collective-permute-done.1.refs_0_, bf16[768,256]{1,0:T(8,128)(2,1)S(1)} %collective-permute-done.4.refs_1_, ...), custom_call_target="tpu_custom_call" | custom-call | tf_op jit(solution)/shard_map/pallas_call | solution.py:104
  32.0 2.1 %collective-permute-done.2.refs_0_ = bf16[384,256]{1,0:T(8,128)(2,1)S(1)} collective-permute-done((bf16[384,256]{1,0:T(8,128)(2,1)S(1)}, bf16[384,256]{1,0:T(8,128)(2,1)S(1)}, u32[]{:S(2)}, u32[]{:S(2)}) %collective-permute-start.2) | collective-permute-done | bytes 196640 | tf_op jit(solution)/shard_map/ppermute | solution.py:18
  34.1 1.4 %collective-permute-start.8 = (bf16[384,256]{1,0:T(8,128)(2,1)S(1)}, bf16[384,256]{1,0:T(8,128)(2,1)S(1)}, u32[]{:S(2)}, u32[]{:S(2)}) collective-permute-start(bf16[384,256]{1,0:T(8,128)(2,1)S(1)} %collective-permute-done.2.refs_0_), channel_id=1, source_target_pairs={{0,2},{1,3},{2,0},{3,1},{4,6},{5,7},{6,4},{7,5},{8,10},{9,11},{10,... | collective-permute-start | bytes 589832 | tf_op jit(solution)/shard_map/ppermute | solution.py:18
  35.7 1.1 %shard_map.105.refs_2_ = f32[768,256]{1,0:T(8,128)S(1)} custom-call(s32[1,8]{1,0:T(1,128)S(1)} %copy-done.1, bf16[384,256]{1,0:T(8,128)(2,1)S(1)} %collective-permute-done.2.refs_0_, bf16[384,256]{1,0:T(8,128)(2,1)S(1)} %collective-permute-done.3.refs_1_, f32[768,256]{1,0:T(8,128)S(1)} %get-tuple-element.32.refs_2_, ...), custom_call_target="tpu_custom_call" | custom-call | tf_op jit(solution)/shard_map/pallas_call | solution.py:104
  37.9 1.5 %collective-permute-start.10 = (bf16[384,256]{1,0:T(8,128)(2,1)S(1)}, bf16[384,256]{1,0:T(8,128)(2,1)S(1)}, u32[]{:S(2)}, u32[]{:S(2)}) collective-permute-start(bf16[384,256]{1,0:T(8,128)(2,1)S(1)} %get-tuple-element.56), channel_id=1, source_target_pairs={{0,1},{1,0},{2,3},{3,2},{4,5},{5,4},{6,7},{7,6},{8,9},{9,8},{10,11... | collective-permute-start | bytes 589832 | tf_op jit(solution)/shard_map/ppermute | solution.py:18
  39.4 3.6 %collective-permute-done.11 = bf16[384,256]{1,0:T(8,128)(2,1)S(1)} collective-permute-done((bf16[384,256]{1,0:T(8,128)(2,1)S(1)}, bf16[384,256]{1,0:T(8,128)(2,1)S(1)}, u32[]{:S(2)}, u32[]{:S(2)}) %collective-permute-start.11) | collective-permute-done | bytes 196640 | tf_op jit(solution)/shard_map/ppermute | solution.py:18
  43.5 4.5 %collective-permute-start.13 = (bf16[384,256]{1,0:T(8,128)(2,1)S(1)}, bf16[384,256]{1,0:T(8,128)(2,1)S(1)}, u32[]{:S(2)}, u32[]{:S(2)}) collective-permute-start(bf16[384,256]{1,0:T(8,128)(2,1)S(1)} %multiply_convert_fusion), channel_id=1, source_target_pairs={{0,16},{3,18},{4,20},{7,22},{8,24},{11,26},{12,28},{15,30},{16,1},... | collective-permute-start | bytes 589832 | tf_op jit(solution)/shard_map/ppermute | solution.py:18
  48.5 3.7 %collective-permute-start.12 = (bf16[384,256]{1,0:T(8,128)(2,1)S(1)}, bf16[384,256]{1,0:T(8,128)(2,1)S(1)}, u32[]{:S(2)}, u32[]{:S(2)}) collective-permute-start(bf16[384,256]{1,0:T(8,128)(2,1)S(1)} %multiply_convert_fusion.1), channel_id=1, source_target_pairs={{0,16},{3,18},{4,20},{7,22},{8,24},{11,26},{12,28},{15,30},{16,1},... | collective-permute-start | bytes 589832 | tf_op jit(solution)/shard_map/ppermute | solution.py:18
  53.0 7.1 %collective-permute-start.15 = (bf16[384,256]{1,0:T(8,128)(2,1)S(1)}, bf16[384,256]{1,0:T(8,128)(2,1)S(1)}, u32[]{:S(2)}, u32[]{:S(2)}) collective-permute-start(bf16[384,256]{1,0:T(8,128)(2,1)S(1)} %broadcast_select_fusion.1.refs_1_), channel_id=1, source_target_pairs={{0,2},{1,3},{2,0},{3,1},{4,6},{5,7},{6,4},{7,5},{8,10},{9,11},{10,... | collective-permute-start | bytes 589832 | tf_op jit(solution)/shard_map/ppermute | solution.py:18
  62.2 1.3 %collective-permute-start.16 = (bf16[384,256]{1,0:T(8,128)(2,1)S(1)}, bf16[384,256]{1,0:T(8,128)(2,1)S(1)}, u32[]{:S(2)}, u32[]{:S(2)}) collective-permute-start(bf16[384,256]{1,0:T(8,128)(2,1)S(1)} %broadcast_select_fusion.2.refs_0_), channel_id=1, source_target_pairs={{0,4},{1,5},{2,10},{3,11},{4,0},{5,1},{6,14},{7,15},{8,12},{9,13},... | collective-permute-start | bytes 589832 | tf_op jit(solution)/shard_map/ppermute | solution.py:18
  63.9 1.2 %collective-permute-done.19.refs_1_ = bf16[384,256]{1,0:T(8,128)(2,1)S(1)} collective-permute-done((bf16[384,256]{1,0:T(8,128)(2,1)S(1)}, bf16[384,256]{1,0:T(8,128)(2,1)S(1)}, u32[]{:S(2)}, u32[]{:S(2)}) %collective-permute-start.19) | collective-permute-done | bytes 196640 | tf_op jit(solution)/shard_map/ppermute | solution.py:18
  65.1 2.9 %collective-permute-start.22 = (bf16[384,256]{1,0:T(8,128)(2,1)S(1)}, bf16[384,256]{1,0:T(8,128)(2,1)S(1)}, u32[]{:S(2)}, u32[]{:S(2)}) collective-permute-start(bf16[384,256]{1,0:T(8,128)(2,1)S(1)} %collective-permute-done.19.refs_1_), channel_id=1, source_target_pairs={{0,2},{1,3},{2,0},{3,1},{4,6},{5,7},{6,4},{7,5},{8,10},{9,11},{10,... | collective-permute-start | bytes 589832 | tf_op jit(solution)/shard_map/ppermute | solution.py:18
  68.1 2.3 %shard_map.107 = (f32[128,128]{1,0:T(8,128)S(1)}, f32[128,128]{1,0:T(8,128)S(1)}) custom-call(s32[256]{0:T(256)S(1)} %select_reduce_fusion.code_ref, s32[5]{0:T(128)S(1)} %convert_reduce_fusion.1.ends_ref, bf16[768,256]{1,0:T(8,128)(2,1)S(1)} %pad_maximum_fusion.emb_ref, bf16[384,256]{1,0:T(8,128)(2,1)S(1)} %broadcast_select_fusion.2.refs_0_, ...), custom_call_target="tpu_custom_call" | custom-call | tf_op jit(solution)/shard_map/pallas_call | solution.py:201
  70.4 1.3 %collective-permute-start.20 = (bf16[384,256]{1,0:T(8,128)(2,1)S(1)}, bf16[384,256]{1,0:T(8,128)(2,1)S(1)}, u32[]{:S(2)}, u32[]{:S(2)}) collective-permute-start(bf16[384,256]{1,0:T(8,128)(2,1)S(1)} %collective-permute-done.19.refs_1_), channel_id=1, source_target_pairs={{0,8},{1,9},{2,6},{3,7},{4,12},{5,13},{6,2},{7,3},{8,0},{9,1},{10,... | collective-permute-start | bytes 589832 | tf_op jit(solution)/shard_map/ppermute | solution.py:18
  74.5 3.8 %shard_map.108 = (f32[128,128]{1,0:T(8,128)S(1)}, f32[128,128]{1,0:T(8,128)S(1)}) custom-call(s32[256]{0:T(256)S(1)} %select_reduce_fusion.code_ref, s32[5]{0:T(128)S(1)} %convert_reduce_fusion.1.ends_ref, bf16[768,256]{1,0:T(8,128)(2,1)S(1)} %pad_maximum_fusion.emb_ref, bf16[384,256]{1,0:T(8,128)(2,1)S(1)} %collective-permute-done.16.refs_0_, ...), custom_call_target="tpu_custom_call" | custom-call | tf_op jit(solution)/shard_map/pallas_call | solution.py:201
  78.9 1.6 %shard_map.109 = (f32[128,128]{1,0:T(8,128)S(1)}, f32[128,128]{1,0:T(8,128)S(1)}) custom-call(s32[256]{0:T(256)S(1)} %select_reduce_fusion.code_ref, s32[5]{0:T(128)S(1)} %convert_reduce_fusion.1.ends_ref, bf16[768,256]{1,0:T(8,128)(2,1)S(1)} %pad_maximum_fusion.emb_ref, bf16[384,256]{1,0:T(8,128)(2,1)S(1)} %collective-permute-done.17.refs_0_, ...), custom_call_target="tpu_custom_call" | custom-call | tf_op jit(solution)/shard_map/pallas_call | solution.py:201
  80.6 2.3 %shard_map.110 = (f32[128,128]{1,0:T(8,128)}, f32[128,128]{1,0:T(8,128)}) custom-call(s32[256]{0:T(256)S(1)} %select_reduce_fusion.code_ref, s32[5]{0:T(128)S(1)} %convert_reduce_fusion.1.ends_ref, bf16[768,256]{1,0:T(8,128)(2,1)S(1)} %pad_maximum_fusion.emb_ref, bf16[384,256]{1,0:T(8,128)(2,1)S(1)} %collective-permute-done.18.refs_0_, ...), custom_call_target="tpu_custom_call" | custom-call | tf_op jit(solution)/shard_map/pallas_call | solution.py:201
  (72 shorter events, 11.9 us)
Async XLA Ops:
  0.7 14.3 %collective-permute-start = (bf16[768,256]{1,0:T(8,128)(2,1)}, bf16[768,256]{1,0:T(8,128)(2,1)S(1)}, u32[]{:S(2)}, u32[]{:S(2)}) collective-permute-start(bf16[768,256]{1,0:T(8,128)(2,1)} %param.8), channel_id=1, source_target_pairs={{0,16},{3,18},{4,20},{7,22},{8,24},{11,26},{12,28},{15,30},{16,1},... | collective-permute-start | bytes 1179656 | tf_op jit(solution)/shard_map/ppermute | solution.py:18
  15.0 7.0 %collective-permute-start.1 = (bf16[768,256]{1,0:T(8,128)(2,1)S(1)}, bf16[768,256]{1,0:T(8,128)(2,1)S(1)}, u32[]{:S(2)}, u32[]{:S(2)}) collective-permute-start(bf16[768,256]{1,0:T(8,128)(2,1)S(1)} %broadcast_select_fusion.refs_0_), channel_id=1, source_target_pairs={{0,4},{1,5},{2,10},{3,11},{4,0},{5,1},{6,14},{7,15},{8,12},{9,13},... | collective-permute-start | bytes 1179656 | tf_op jit(solution)/shard_map/ppermute | solution.py:18
  15.6 11.5 %collective-permute-start.5 = (bf16[768,256]{1,0:T(8,128)(2,1)S(1)}, bf16[768,256]{1,0:T(8,128)(2,1)S(1)}, u32[]{:S(2)}, u32[]{:S(2)}) collective-permute-start(bf16[768,256]{1,0:T(8,128)(2,1)S(1)} %broadcast_select_fusion.refs_0_), channel_id=1, source_target_pairs={{0,8},{1,9},{2,6},{3,7},{4,12},{5,13},{6,2},{7,3},{8,0},{9,1},{10,... | collective-permute-start | bytes 1179656 | tf_op jit(solution)/shard_map/ppermute | solution.py:18
  16.8 12.2 %collective-permute-start.7 = (bf16[768,256]{1,0:T(8,128)(2,1)S(1)}, bf16[768,256]{1,0:T(8,128)(2,1)S(1)}, u32[]{:S(2)}, u32[]{:S(2)}) collective-permute-start(bf16[768,256]{1,0:T(8,128)(2,1)S(1)} %broadcast_select_fusion.refs_0_), channel_id=1, source_target_pairs={{0,2},{1,3},{2,0},{3,1},{4,6},{5,7},{6,4},{7,5},{8,10},{9,11},{10,... | collective-permute-start | bytes 1179656 | tf_op jit(solution)/shard_map/ppermute | solution.py:18
  22.0 7.7 %collective-permute-start.4 = (bf16[768,256]{1,0:T(8,128)(2,1)S(1)}, bf16[768,256]{1,0:T(8,128)(2,1)S(1)}, u32[]{:S(2)}, u32[]{:S(2)}) collective-permute-start(bf16[768,256]{1,0:T(8,128)(2,1)S(1)} %collective-permute-done.1.refs_0_), channel_id=1, source_target_pairs={{0,2},{1,3},{2,0},{3,1},{4,6},{5,7},{6,4},{7,5},{8,10},{9,11},{10,... | collective-permute-start | bytes 1179656 | tf_op jit(solution)/shard_map/ppermute | solution.py:18
  27.1 2.6 %collective-permute-start.6 = (bf16[768,256]{1,0:T(8,128)(2,1)S(1)}, bf16[768,256]{1,0:T(8,128)(2,1)S(1)}, u32[]{:S(2)}, u32[]{:S(2)}) collective-permute-start(bf16[768,256]{1,0:T(8,128)(2,1)S(1)} %collective-permute-done.5.refs_2_), channel_id=1, source_target_pairs={{0,2},{1,3},{2,0},{3,1},{4,6},{5,7},{6,4},{7,5},{8,10},{9,11},{10,... | collective-permute-start | bytes 1179656 | tf_op jit(solution)/shard_map/ppermute | solution.py:18
  27.1 4.9 %collective-permute-start.3 = (bf16[384,256]{1,0:T(8,128)(2,1)S(1)}, bf16[384,256]{1,0:T(8,128)(2,1)S(1)}, u32[]{:S(2)}, u32[]{:S(2)}) collective-permute-start(bf16[384,256]{1,0:T(8,128)(2,1)S(1)} %get-tuple-element.57), channel_id=1, source_target_pairs={{0,8},{1,9},{2,6},{3,7},{4,12},{5,13},{6,2},{7,3},{8,0},{9,1},{10,... | collective-permute-start | bytes 589832 | tf_op jit(solution)/shard_map/ppermute | solution.py:18
  28.4 5.7 %collective-permute-start.2 = (bf16[384,256]{1,0:T(8,128)(2,1)S(1)}, bf16[384,256]{1,0:T(8,128)(2,1)S(1)}, u32[]{:S(2)}, u32[]{:S(2)}) collective-permute-start(bf16[384,256]{1,0:T(8,128)(2,1)S(1)} %get-tuple-element.58), channel_id=1, source_target_pairs={{0,8},{1,9},{2,6},{3,7},{4,12},{5,13},{6,2},{7,3},{8,0},{9,1},{10,... | collective-permute-start | bytes 589832 | tf_op jit(solution)/shard_map/ppermute | solution.py:18
  34.1 2.8 %collective-permute-start.8 = (bf16[384,256]{1,0:T(8,128)(2,1)S(1)}, bf16[384,256]{1,0:T(8,128)(2,1)S(1)}, u32[]{:S(2)}, u32[]{:S(2)}) collective-permute-start(bf16[384,256]{1,0:T(8,128)(2,1)S(1)} %collective-permute-done.2.refs_0_), channel_id=1, source_target_pairs={{0,2},{1,3},{2,0},{3,1},{4,6},{5,7},{6,4},{7,5},{8,10},{9,11},{10,... | collective-permute-start | bytes 589832 | tf_op jit(solution)/shard_map/ppermute | solution.py:18
  37.6 5.4 %collective-permute-start.11 = (bf16[384,256]{1,0:T(8,128)(2,1)S(1)}, bf16[384,256]{1,0:T(8,128)(2,1)S(1)}, u32[]{:S(2)}, u32[]{:S(2)}) collective-permute-start(bf16[384,256]{1,0:T(8,128)(2,1)S(1)} %get-tuple-element.55), channel_id=1, source_target_pairs={{0,1},{1,0},{2,3},{3,2},{4,5},{5,4},{6,7},{7,6},{8,9},{9,8},{10,11... | collective-permute-start | bytes 589832 | tf_op jit(solution)/shard_map/ppermute | solution.py:18
  37.9 10.2 %collective-permute-start.10 = (bf16[384,256]{1,0:T(8,128)(2,1)S(1)}, bf16[384,256]{1,0:T(8,128)(2,1)S(1)}, u32[]{:S(2)}, u32[]{:S(2)}) collective-permute-start(bf16[384,256]{1,0:T(8,128)(2,1)S(1)} %get-tuple-element.56), channel_id=1, source_target_pairs={{0,1},{1,0},{2,3},{3,2},{4,5},{5,4},{6,7},{7,6},{8,9},{9,8},{10,11... | collective-permute-start | bytes 589832 | tf_op jit(solution)/shard_map/ppermute | solution.py:18
  43.5 9.4 %collective-permute-start.13 = (bf16[384,256]{1,0:T(8,128)(2,1)S(1)}, bf16[384,256]{1,0:T(8,128)(2,1)S(1)}, u32[]{:S(2)}, u32[]{:S(2)}) collective-permute-start(bf16[384,256]{1,0:T(8,128)(2,1)S(1)} %multiply_convert_fusion), channel_id=1, source_target_pairs={{0,16},{3,18},{4,20},{7,22},{8,24},{11,26},{12,28},{15,30},{16,1},... | collective-permute-start | bytes 589832 | tf_op jit(solution)/shard_map/ppermute | solution.py:18
  48.5 12.7 %collective-permute-start.12 = (bf16[384,256]{1,0:T(8,128)(2,1)S(1)}, bf16[384,256]{1,0:T(8,128)(2,1)S(1)}, u32[]{:S(2)}, u32[]{:S(2)}) collective-permute-start(bf16[384,256]{1,0:T(8,128)(2,1)S(1)} %multiply_convert_fusion.1), channel_id=1, source_target_pairs={{0,16},{3,18},{4,20},{7,22},{8,24},{11,26},{12,28},{15,30},{16,1},... | collective-permute-start | bytes 589832 | tf_op jit(solution)/shard_map/ppermute | solution.py:18
  53.0 10.5 %collective-permute-start.15 = (bf16[384,256]{1,0:T(8,128)(2,1)S(1)}, bf16[384,256]{1,0:T(8,128)(2,1)S(1)}, u32[]{:S(2)}, u32[]{:S(2)}) collective-permute-start(bf16[384,256]{1,0:T(8,128)(2,1)S(1)} %broadcast_select_fusion.1.refs_1_), channel_id=1, source_target_pairs={{0,2},{1,3},{2,0},{3,1},{4,6},{5,7},{6,4},{7,5},{8,10},{9,11},{10,... | collective-permute-start | bytes 589832 | tf_op jit(solution)/shard_map/ppermute | solution.py:18
  60.1 4.9 %collective-permute-start.19 = (bf16[384,256]{1,0:T(8,128)(2,1)S(1)}, bf16[384,256]{1,0:T(8,128)(2,1)S(1)}, u32[]{:S(2)}, u32[]{:S(2)}) collective-permute-start(bf16[384,256]{1,0:T(8,128)(2,1)S(1)} %broadcast_select_fusion.1.refs_1_), channel_id=1, source_target_pairs={{0,4},{1,5},{2,10},{3,11},{4,0},{5,1},{6,14},{7,15},{8,12},{9,13},... | collective-permute-start | bytes 589832 | tf_op jit(solution)/shard_map/ppermute | solution.py:18
  60.1 11.5 %collective-permute-start.24 = (bf16[384,256]{1,0:T(8,128)(2,1)S(1)}, bf16[384,256]{1,0:T(8,128)(2,1)S(1)}, u32[]{:S(2)}, u32[]{:S(2)}) collective-permute-start(bf16[384,256]{1,0:T(8,128)(2,1)S(1)} %broadcast_select_fusion.1.refs_1_), channel_id=1, source_target_pairs={{0,8},{1,9},{2,6},{3,7},{4,12},{5,13},{6,2},{7,3},{8,0},{9,1},{10,... | collective-permute-start | bytes 589832 | tf_op jit(solution)/shard_map/ppermute | solution.py:18
  61.4 6.7 %collective-permute-start.14 = (bf16[384,256]{1,0:T(8,128)(2,1)S(1)}, bf16[384,256]{1,0:T(8,128)(2,1)S(1)}, u32[]{:S(2)}, u32[]{:S(2)}) collective-permute-start(bf16[384,256]{1,0:T(8,128)(2,1)S(1)} %broadcast_select_fusion.2.refs_0_), channel_id=1, source_target_pairs={{0,2},{1,3},{2,0},{3,1},{4,6},{5,7},{6,4},{7,5},{8,10},{9,11},{10,... | collective-permute-start | bytes 589832 | tf_op jit(solution)/shard_map/ppermute | solution.py:18
  62.2 9.4 %collective-permute-start.16 = (bf16[384,256]{1,0:T(8,128)(2,1)S(1)}, bf16[384,256]{1,0:T(8,128)(2,1)S(1)}, u32[]{:S(2)}, u32[]{:S(2)}) collective-permute-start(bf16[384,256]{1,0:T(8,128)(2,1)S(1)} %broadcast_select_fusion.2.refs_0_), channel_id=1, source_target_pairs={{0,4},{1,5},{2,10},{3,11},{4,0},{5,1},{6,14},{7,15},{8,12},{9,13},... | collective-permute-start | bytes 589832 | tf_op jit(solution)/shard_map/ppermute | solution.py:18
  63.5 9.2 %collective-permute-start.23 = (bf16[384,256]{1,0:T(8,128)(2,1)S(1)}, bf16[384,256]{1,0:T(8,128)(2,1)S(1)}, u32[]{:S(2)}, u32[]{:S(2)}) collective-permute-start(bf16[384,256]{1,0:T(8,128)(2,1)S(1)} %broadcast_select_fusion.2.refs_0_), channel_id=1, source_target_pairs={{0,8},{1,9},{2,6},{3,7},{4,12},{5,13},{6,2},{7,3},{8,0},{9,1},{10,... | collective-permute-start | bytes 589832 | tf_op jit(solution)/shard_map/ppermute | solution.py:18
  65.1 7.7 %collective-permute-start.22 = (bf16[384,256]{1,0:T(8,128)(2,1)S(1)}, bf16[384,256]{1,0:T(8,128)(2,1)S(1)}, u32[]{:S(2)}, u32[]{:S(2)}) collective-permute-start(bf16[384,256]{1,0:T(8,128)(2,1)S(1)} %collective-permute-done.19.refs_1_), channel_id=1, source_target_pairs={{0,2},{1,3},{2,0},{3,1},{4,6},{5,7},{6,4},{7,5},{8,10},{9,11},{10,... | collective-permute-start | bytes 589832 | tf_op jit(solution)/shard_map/ppermute | solution.py:18
  70.4 7.9 %collective-permute-start.20 = (bf16[384,256]{1,0:T(8,128)(2,1)S(1)}, bf16[384,256]{1,0:T(8,128)(2,1)S(1)}, u32[]{:S(2)}, u32[]{:S(2)}) collective-permute-start(bf16[384,256]{1,0:T(8,128)(2,1)S(1)} %collective-permute-done.19.refs_1_), channel_id=1, source_target_pairs={{0,8},{1,9},{2,6},{3,7},{4,12},{5,13},{6,2},{7,3},{8,0},{9,1},{10,... | collective-permute-start | bytes 589832 | tf_op jit(solution)/shard_map/ppermute | solution.py:18
  71.7 2.6 %collective-permute-start.21 = (bf16[384,256]{1,0:T(8,128)(2,1)S(1)}, bf16[384,256]{1,0:T(8,128)(2,1)S(1)}, u32[]{:S(2)}, u32[]{:S(2)}) collective-permute-start(bf16[384,256]{1,0:T(8,128)(2,1)S(1)} %collective-permute-done.16.refs_0_), channel_id=1, source_target_pairs={{0,2},{1,3},{2,0},{3,1},{4,6},{5,7},{6,4},{7,5},{8,10},{9,11},{10,... | collective-permute-start | bytes 589832 | tf_op jit(solution)/shard_map/ppermute | solution.py:18
  71.7 7.0 %collective-permute-start.17 = (bf16[384,256]{1,0:T(8,128)(2,1)S(1)}, bf16[384,256]{1,0:T(8,128)(2,1)S(1)}, u32[]{:S(2)}, u32[]{:S(2)}) collective-permute-start(bf16[384,256]{1,0:T(8,128)(2,1)S(1)} %collective-permute-done.16.refs_0_), channel_id=1, source_target_pairs={{0,8},{1,9},{2,6},{3,7},{4,12},{5,13},{6,2},{7,3},{8,0},{9,1},{10,... | collective-permute-start | bytes 589832 | tf_op jit(solution)/shard_map/ppermute | solution.py:18
  78.3 2.2 %collective-permute-start.27 = (bf16[384,256]{1,0:T(8,128)(2,1)S(1)}, bf16[384,256]{1,0:T(8,128)(2,1)S(1)}, u32[]{:S(2)}, u32[]{:S(2)}) collective-permute-start(bf16[384,256]{1,0:T(8,128)(2,1)S(1)} %collective-permute-done.20.refs_1_), channel_id=1, source_target_pairs={{0,2},{1,3},{2,0},{3,1},{4,6},{5,7},{6,4},{7,5},{8,10},{9,11},{10,... | collective-permute-start | bytes 589832 | tf_op jit(solution)/shard_map/ppermute | solution.py:18
  (9 other events, 94.9 us)

commit v3 on v2

--- a/solution.py
+++ b/solution.py
@@ -130,9 +130,13 @@
     return out[0], out[1:]
 
 
-def score_kernel(n_arrays, places, which, has_previous, code_ref, ends_ref, emb_ref, *refs):
+def score_kernel(n_arrays, places, which, has_previous, write_rows, code_ref, ends_ref, emb_ref, *refs):
     key_refs, refs = refs[:n_arrays], refs[n_arrays:]
     previous_refs, refs = (refs[:2], refs[2:]) if has_previous else (None, refs)
+    if write_rows:
+        rows_ref, refs = refs[0], refs[1:]
+        first = pl.multiple_of(lax.axis_index("rep") * write_rows, PAIR_ROWS)
+        rows_ref[...] = emb_ref[pl.ds(first, write_rows), :]
     pos_ref, neg_ref, scores, losses = refs
     blocksize, channels = emb_ref.shape
     n_pairs = pos_ref.shape[0]
@@ -192,21 +196,22 @@
     neg_ref[...] = losses[n_pairs:, :]
 
 
-def score_pairs(codes, ends, which, embedding_block, blocks, n_pairs, previous):
+def score_pairs(codes, ends, which, embedding_block, blocks, n_pairs, previous, write_rows=0):
     blocksize, channels = embedding_block.shape
     n_rows = len(blocks) * blocksize
     loss = jax.ShapeDtypeStruct((n_pairs, PAIR_ROWS), jnp.float32)
+    rows = [jax.ShapeDtypeStruct((write_rows, channels), jnp.bfloat16)] if write_rows else []
     arrays, places = plan(blocks)
     extra = [] if previous is None else list(previous)
     return pl.pallas_call(
-        functools.partial(score_kernel, len(arrays), places, which, previous is not None),
+        functools.partial(score_kernel, len(arrays), places, which, previous is not None, write_rows),
         in_specs=[pl.BlockSpec(memory_space=pltpu.SMEM)] * 2 + vmem(1 + len(arrays) + len(extra)),
-        out_specs=vmem(2),
+        out_specs=vmem(2 + len(rows)),
         scratch_shapes=[
             pltpu.VMEM((blocksize // PAIR_ROWS, n_rows + EDGE, PAIR_ROWS), jnp.float32),
             pltpu.VMEM((2 * n_pairs, PAIR_ROWS), jnp.float32),
         ],
-        out_shape=[loss, loss],
+        out_shape=rows + [loss, loss],
         compiler_params=pltpu.CompilerParams(vmem_limit_bytes=24 * 1024 * 1024),
     )(codes, ends, embedding_block, *arrays, *extra)
 
@@ -358,13 +363,17 @@
     scored, output = [], []
 
     def score(queries, blocks, earlier):
+        limits = ends
         if len(scored) == 1:
-            own_now, earlier = lax.optimization_barrier((own, earlier))
-            rows = jnp.where(rep == 0, own_now[0], own_now[1])
-            rows, earlier = lax.optimization_barrier((rows, earlier))
-            output.append(rows)
+            limits, earlier = lax.optimization_barrier((ends, earlier))
+            limits, earlier = lax.optimization_barrier((jnp.maximum(limits, 0), earlier))
         scored.append(len(blocks))
-        return score_pairs(codes, ends, len(scored) - 1, queries, blocks, n_pairs, earlier)
+        write_rows = share if spread.halved and len(scored) == 1 else 0
+        *rows, pos_loss, neg_loss = score_pairs(
+            codes, limits, len(scored) - 1, queries, blocks, n_pairs, earlier, write_rows
+        )
+        output.extend(rows)
+        return pos_loss, neg_loss
 
     if spread.halved:
         block = jnp.concatenate(own, axis=0)

time: 83.1 us -> 83.3 us (level)
  Pallas kernels: 14.3 us -> 17.2 us
  starting transfers between devices: 43.4 us -> 41.7 us
    pallas_call x4, Pallas kernels: 4.27 us -> 6.51 us  [aggregate(): pl.pallas_call(functools.partial(aggregate_kernel, len(arrays), places, m...]
    ppermute x28, starting transfers between devices: 43.4 us -> 41.7 us  [permute(): lax.ppermute(block, ('row', 'rep'), [(a[0] * n_rep + a[1], b[0] * n_rep +...]
  transfers between devices with their start and end apart: 28 -> 28, of which waited for: 9 -> 8; matrix products, arithmetic and copies ran while one was open for 4% -> 3% of each run, Pallas kernels for 14% -> 17%
where the time goes in v3:
time: 83.3 us; the launch traced here: 82.8 us
  starting transfers between devices  41.7 us (50%)
  waiting for transfers between devices  20.1 us (24%)
  Pallas kernels  17.2 us (21%)
  matrix products  1.05 us (1%)
  other arithmetic  1.02 us (1%)
  between operations  0.98 us (1%)
    ppermute x28, starting transfers between devices, permute(): lax.ppermute(block, ('row', 'rep'), [(a[0] * n_rep + a[1], b[0] * n_rep +...  41.7 us
    ppermute x28, waiting for transfers between devices, permute(): lax.ppermute(block, ('row', 'rep'), [(a[0] * n_rep + a[1], b[0] * n_rep +...  20.1 us
    pallas_call x4, Pallas kernels, score_pairs(): pl.pallas_call(functools.partial(score_kernel, len(arrays), places, which...  10.7 us
    pallas_call x4, Pallas kernels, aggregate(): pl.pallas_call(functools.partial(aggregate_kernel, len(arrays), places, m...  6.51 us
  transfers between devices with their start and end apart: 28, of which 8 were waited for; matrix products, arithmetic and copies ran while one was open for 3% of the time, Pallas kernels for 17%

profile of v3, /device:TPU:3, one launch (start us, length us, event | category | flops | bytes accessed | tf_op | source)
XLA Modules:
  0.0 82.8 jit_solution(3819993171042234046)
XLA Ops:
  0.7 4.3 %collective-permute-start = (bf16[768,256]{1,0:T(8,128)(2,1)}, bf16[768,256]{1,0:T(8,128)(2,1)S(1)}, u32[]{:S(2)}, u32[]{:S(2)}) collective-permute-start(bf16[768,256]{1,0:T(8,128)(2,1)} %param.8), channel_id=1, source_target_pairs={{0,16},{3,18},{4,20},{7,22},{8,24},{11,26},{12,28},{15,30},{16,1},... | collective-permute-start | bytes 1179656 | tf_op jit(solution)/shard_map/ppermute | solution.py:18
  5.7 9.2 %collective-permute-done = bf16[768,256]{1,0:T(8,128)(2,1)S(1)} collective-permute-done((bf16[768,256]{1,0:T(8,128)(2,1)}, bf16[768,256]{1,0:T(8,128)(2,1)S(1)}, u32[]{:S(2)}, u32[]{:S(2)}) %collective-permute-start) | collective-permute-done | bytes 393248 | tf_op jit(solution)/shard_map/ppermute | solution.py:18
  15.6 1.2 %collective-permute-start.5 = (bf16[768,256]{1,0:T(8,128)(2,1)S(1)}, bf16[768,256]{1,0:T(8,128)(2,1)S(1)}, u32[]{:S(2)}, u32[]{:S(2)}) collective-permute-start(bf16[768,256]{1,0:T(8,128)(2,1)S(1)} %broadcast_select_fusion.refs_0_), channel_id=1, source_target_pairs={{0,8},{1,9},{2,6},{3,7},{4,12},{5,13},{6,2},{7,3},{8,0},{9,1},{10,... | collective-permute-start | bytes 1179656 | tf_op jit(solution)/shard_map/ppermute | solution.py:18
  16.8 2.3 %collective-permute-start.7 = (bf16[768,256]{1,0:T(8,128)(2,1)S(1)}, bf16[768,256]{1,0:T(8,128)(2,1)S(1)}, u32[]{:S(2)}, u32[]{:S(2)}) collective-permute-start(bf16[768,256]{1,0:T(8,128)(2,1)S(1)} %broadcast_select_fusion.refs_0_), channel_id=1, source_target_pairs={{0,2},{1,3},{2,0},{3,1},{4,6},{5,7},{6,4},{7,5},{8,10},{9,11},{10,... | collective-permute-start | bytes 1179656 | tf_op jit(solution)/shard_map/ppermute | solution.py:18
  19.1 2.8 %collective-permute-done.1.refs_0_ = bf16[768,256]{1,0:T(8,128)(2,1)S(1)} collective-permute-done((bf16[768,256]{1,0:T(8,128)(2,1)S(1)}, bf16[768,256]{1,0:T(8,128)(2,1)S(1)}, u32[]{:S(2)}, u32[]{:S(2)}) %collective-permute-start.1) | collective-permute-done | bytes 393248 | tf_op jit(solution)/shard_map/ppermute | solution.py:18
  22.0 5.1 %collective-permute-start.4 = (bf16[768,256]{1,0:T(8,128)(2,1)S(1)}, bf16[768,256]{1,0:T(8,128)(2,1)S(1)}, u32[]{:S(2)}, u32[]{:S(2)}) collective-permute-start(bf16[768,256]{1,0:T(8,128)(2,1)S(1)} %collective-permute-done.1.refs_0_), channel_id=1, source_target_pairs={{0,2},{1,3},{2,0},{3,1},{4,6},{5,7},{6,4},{7,5},{8,10},{9,11},{10,... | collective-permute-start | bytes 1179656 | tf_op jit(solution)/shard_map/ppermute | solution.py:18
  27.1 1.3 %collective-permute-start.3 = (bf16[384,256]{1,0:T(8,128)(2,1)S(1)}, bf16[384,256]{1,0:T(8,128)(2,1)S(1)}, u32[]{:S(2)}, u32[]{:S(2)}) collective-permute-start(bf16[384,256]{1,0:T(8,128)(2,1)S(1)} %get-tuple-element.57), channel_id=1, source_target_pairs={{0,8},{1,9},{2,6},{3,7},{4,12},{5,13},{6,2},{7,3},{8,0},{9,1},{10,... | collective-permute-start | bytes 589832 | tf_op jit(solution)/shard_map/ppermute | solution.py:18
  29.0 2.4 %shard_map.103.refs_4_ = f32[768,256]{1,0:T(8,128)S(1)} custom-call(s32[1,8]{1,0:T(1,128)S(1)} %copy-done.1, bf16[768,256]{1,0:T(8,128)(2,1)S(1)} %broadcast_select_fusion.refs_0_, bf16[768,256]{1,0:T(8,128)(2,1)S(1)} %collective-permute-done.7.refs_1_, bf16[768,6144]{1,0:T(8,128)(2,1)} %refs_5_.1), custom_call_target="tpu_custom_call" | custom-call | tf_op jit(solution)/shard_map/pallas_call | solution.py:104
  31.4 2.4 %shard_map.104 = (f32[768,256]{1,0:T(8,128)S(1)}, bf16[768,768]{1,0:T(8,128)(2,1)S(1)}, bf16[768,768]{1,0:T(8,128)(2,1)S(1)}) custom-call(s32[1,8]{1,0:T(1,128)S(1)} %copy-done.1, bf16[768,256]{1,0:T(8,128)(2,1)S(1)} %collective-permute-done.1.refs_0_, bf16[768,256]{1,0:T(8,128)(2,1)S(1)} %collective-permute-done.4.refs_1_, ...), custom_call_target="tpu_custom_call" | custom-call | tf_op jit(solution)/shard_map/pallas_call | solution.py:104
  34.1 1.4 %collective-permute-start.8 = (bf16[384,256]{1,0:T(8,128)(2,1)S(1)}, bf16[384,256]{1,0:T(8,128)(2,1)S(1)}, u32[]{:S(2)}, u32[]{:S(2)}) collective-permute-start(bf16[384,256]{1,0:T(8,128)(2,1)S(1)} %collective-permute-done.2.refs_0_), channel_id=1, source_target_pairs={{0,2},{1,3},{2,0},{3,1},{4,6},{5,7},{6,4},{7,5},{8,10},{9,11},{10,... | collective-permute-start | bytes 589832 | tf_op jit(solution)/shard_map/ppermute | solution.py:18
  37.9 1.5 %collective-permute-start.10 = (bf16[384,256]{1,0:T(8,128)(2,1)S(1)}, bf16[384,256]{1,0:T(8,128)(2,1)S(1)}, u32[]{:S(2)}, u32[]{:S(2)}) collective-permute-start(bf16[384,256]{1,0:T(8,128)(2,1)S(1)} %get-tuple-element.55), channel_id=1, source_target_pairs={{0,1},{1,0},{2,3},{3,2},{4,5},{5,4},{6,7},{7,6},{8,9},{9,8},{10,11... | collective-permute-start | bytes 589832 | tf_op jit(solution)/shard_map/ppermute | solution.py:18
  39.4 3.8 %collective-permute-done.11 = bf16[384,256]{1,0:T(8,128)(2,1)S(1)} collective-permute-done((bf16[384,256]{1,0:T(8,128)(2,1)S(1)}, bf16[384,256]{1,0:T(8,128)(2,1)S(1)}, u32[]{:S(2)}, u32[]{:S(2)}) %collective-permute-start.11) | collective-permute-done | bytes 196640 | tf_op jit(solution)/shard_map/ppermute | solution.py:18
  43.7 3.7 %collective-permute-start.13 = (bf16[384,256]{1,0:T(8,128)(2,1)S(1)}, bf16[384,256]{1,0:T(8,128)(2,1)S(1)}, u32[]{:S(2)}, u32[]{:S(2)}) collective-permute-start(bf16[384,256]{1,0:T(8,128)(2,1)S(1)} %multiply_convert_fusion), channel_id=1, source_target_pairs={{0,16},{3,18},{4,20},{7,22},{8,24},{11,26},{12,28},{15,30},{16,1},... | collective-permute-start | bytes 589832 | tf_op jit(solution)/shard_map/ppermute | solution.py:18
  47.9 3.7 %collective-permute-start.12 = (bf16[384,256]{1,0:T(8,128)(2,1)S(1)}, bf16[384,256]{1,0:T(8,128)(2,1)S(1)}, u32[]{:S(2)}, u32[]{:S(2)}) collective-permute-start(bf16[384,256]{1,0:T(8,128)(2,1)S(1)} %multiply_convert_fusion.1), channel_id=1, source_target_pairs={{0,16},{3,18},{4,20},{7,22},{8,24},{11,26},{12,28},{15,30},{16,1},... | collective-permute-start | bytes 589832 | tf_op jit(solution)/shard_map/ppermute | solution.py:18
  51.6 1.5 %collective-permute-done.13 = bf16[384,256]{1,0:T(8,128)(2,1)S(1)} collective-permute-done((bf16[384,256]{1,0:T(8,128)(2,1)S(1)}, bf16[384,256]{1,0:T(8,128)(2,1)S(1)}, u32[]{:S(2)}, u32[]{:S(2)}) %collective-permute-start.13) | collective-permute-done | bytes 196640 | tf_op jit(solution)/shard_map/ppermute | solution.py:18
  53.2 6.7 %collective-permute-start.15 = (bf16[384,256]{1,0:T(8,128)(2,1)S(1)}, bf16[384,256]{1,0:T(8,128)(2,1)S(1)}, u32[]{:S(2)}, u32[]{:S(2)}) collective-permute-start(bf16[384,256]{1,0:T(8,128)(2,1)S(1)} %broadcast_select_fusion.1.refs_1_), channel_id=1, source_target_pairs={{0,2},{1,3},{2,0},{3,1},{4,6},{5,7},{6,4},{7,5},{8,10},{9,11},{10,... | collective-permute-start | bytes 589832 | tf_op jit(solution)/shard_map/ppermute | solution.py:18
  60.0 1.2 %collective-permute-start.24 = (bf16[384,256]{1,0:T(8,128)(2,1)S(1)}, bf16[384,256]{1,0:T(8,128)(2,1)S(1)}, u32[]{:S(2)}, u32[]{:S(2)}) collective-permute-start(bf16[384,256]{1,0:T(8,128)(2,1)S(1)} %broadcast_select_fusion.1.refs_1_), channel_id=1, source_target_pairs={{0,8},{1,9},{2,6},{3,7},{4,12},{5,13},{6,2},{7,3},{8,0},{9,1},{10,... | collective-permute-start | bytes 589832 | tf_op jit(solution)/shard_map/ppermute | solution.py:18
  62.1 1.4 %collective-permute-start.16 = (bf16[384,256]{1,0:T(8,128)(2,1)S(1)}, bf16[384,256]{1,0:T(8,128)(2,1)S(1)}, u32[]{:S(2)}, u32[]{:S(2)}) collective-permute-start(bf16[384,256]{1,0:T(8,128)(2,1)S(1)} %broadcast_select_fusion.2.refs_0_), channel_id=1, source_target_pairs={{0,4},{1,5},{2,10},{3,11},{4,0},{5,1},{6,14},{7,15},{8,12},{9,13},... | collective-permute-start | bytes 589832 | tf_op jit(solution)/shard_map/ppermute | solution.py:18
  64.8 3.0 %collective-permute-start.22 = (bf16[384,256]{1,0:T(8,128)(2,1)S(1)}, bf16[384,256]{1,0:T(8,128)(2,1)S(1)}, u32[]{:S(2)}, u32[]{:S(2)}) collective-permute-start(bf16[384,256]{1,0:T(8,128)(2,1)S(1)} %collective-permute-done.19.refs_1_), channel_id=1, source_target_pairs={{0,2},{1,3},{2,0},{3,1},{4,6},{5,7},{6,4},{7,5},{8,10},{9,11},{10,... | collective-permute-start | bytes 589832 | tf_op jit(solution)/shard_map/ppermute | solution.py:18
  67.9 3.0 %shard_map.107 = (bf16[384,256]{1,0:T(8,128)(2,1)}, f32[128,128]{1,0:T(8,128)S(1)}, f32[128,128]{1,0:T(8,128)S(1)}) custom-call(s32[256]{0:T(256)S(1)} %select_reduce_fusion.code_ref, s32[5]{0:T(128)S(1)} %convert_reduce_fusion.1.ends_ref, bf16[768,256]{1,0:T(8,128)(2,1)S(1)} %pad_maximum_fusion.emb_ref, ...), custom_call_target="tpu_custom_call" | custom-call | tf_op jit(solution)/shard_map/pallas_call | solution.py:206
  70.9 1.4 %collective-permute-start.20 = (bf16[384,256]{1,0:T(8,128)(2,1)S(1)}, bf16[384,256]{1,0:T(8,128)(2,1)S(1)}, u32[]{:S(2)}, u32[]{:S(2)}) collective-permute-start(bf16[384,256]{1,0:T(8,128)(2,1)S(1)} %collective-permute-done.19.refs_1_), channel_id=1, source_target_pairs={{0,8},{1,9},{2,6},{3,7},{4,12},{5,13},{6,2},{7,3},{8,0},{9,1},{10,... | collective-permute-start | bytes 589832 | tf_op jit(solution)/shard_map/ppermute | solution.py:18
  74.5 3.9 %shard_map.108 = (f32[128,128]{1,0:T(8,128)S(1)}, f32[128,128]{1,0:T(8,128)S(1)}) custom-call(s32[256]{0:T(256)S(1)} %select_reduce_fusion.code_ref, s32[5]{0:T(128)S(1)} %broadcast_maximum_fusion.ends_ref, bf16[768,256]{1,0:T(8,128)(2,1)S(1)} %pad_maximum_fusion.emb_ref, bf16[384,256]{1,0:T(8,128)(2,1)S(1)} %collective-permute-done.16.refs_0_, ...), custom_call_target="tpu_custom_call" | custom-call | tf_op jit(solution)/shard_map/pallas_call | solution.py:206
  79.0 1.5 %shard_map.109 = (f32[128,128]{1,0:T(8,128)S(1)}, f32[128,128]{1,0:T(8,128)S(1)}) custom-call(s32[256]{0:T(256)S(1)} %select_reduce_fusion.code_ref, s32[5]{0:T(128)S(1)} %convert_reduce_fusion.1.ends_ref, bf16[768,256]{1,0:T(8,128)(2,1)S(1)} %pad_maximum_fusion.emb_ref, bf16[384,256]{1,0:T(8,128)(2,1)S(1)} %collective-permute-done.17.refs_0_, ...), custom_call_target="tpu_custom_call" | custom-call | tf_op jit(solution)/shard_map/pallas_call | solution.py:206
  80.5 2.3 %shard_map.110 = (f32[128,128]{1,0:T(8,128)}, f32[128,128]{1,0:T(8,128)}) custom-call(s32[256]{0:T(256)S(1)} %select_reduce_fusion.code_ref, s32[5]{0:T(128)S(1)} %convert_reduce_fusion.1.ends_ref, bf16[768,256]{1,0:T(8,128)(2,1)S(1)} %pad_maximum_fusion.emb_ref, bf16[384,256]{1,0:T(8,128)(2,1)S(1)} %collective-permute-done.18.refs_0_, ...), custom_call_target="tpu_custom_call" | custom-call | tf_op jit(solution)/shard_map/pallas_call | solution.py:206
  (72 shorter events, 10.7 us)
Async XLA Ops:
  0.7 14.3 %collective-permute-start = (bf16[768,256]{1,0:T(8,128)(2,1)}, bf16[768,256]{1,0:T(8,128)(2,1)S(1)}, u32[]{:S(2)}, u32[]{:S(2)}) collective-permute-start(bf16[768,256]{1,0:T(8,128)(2,1)} %param.8), channel_id=1, source_target_pairs={{0,16},{3,18},{4,20},{7,22},{8,24},{11,26},{12,28},{15,30},{16,1},... | collective-permute-start | bytes 1179656 | tf_op jit(solution)/shard_map/ppermute | solution.py:18
  15.0 7.0 %collective-permute-start.1 = (bf16[768,256]{1,0:T(8,128)(2,1)S(1)}, bf16[768,256]{1,0:T(8,128)(2,1)S(1)}, u32[]{:S(2)}, u32[]{:S(2)}) collective-permute-start(bf16[768,256]{1,0:T(8,128)(2,1)S(1)} %broadcast_select_fusion.refs_0_), channel_id=1, source_target_pairs={{0,4},{1,5},{2,10},{3,11},{4,0},{5,1},{6,14},{7,15},{8,12},{9,13},... | collective-permute-start | bytes 1179656 | tf_op jit(solution)/shard_map/ppermute | solution.py:18
  15.6 11.5 %collective-permute-start.5 = (bf16[768,256]{1,0:T(8,128)(2,1)S(1)}, bf16[768,256]{1,0:T(8,128)(2,1)S(1)}, u32[]{:S(2)}, u32[]{:S(2)}) collective-permute-start(bf16[768,256]{1,0:T(8,128)(2,1)S(1)} %broadcast_select_fusion.refs_0_), channel_id=1, source_target_pairs={{0,8},{1,9},{2,6},{3,7},{4,12},{5,13},{6,2},{7,3},{8,0},{9,1},{10,... | collective-permute-start | bytes 1179656 | tf_op jit(solution)/shard_map/ppermute | solution.py:18
  16.8 12.2 %collective-permute-start.7 = (bf16[768,256]{1,0:T(8,128)(2,1)S(1)}, bf16[768,256]{1,0:T(8,128)(2,1)S(1)}, u32[]{:S(2)}, u32[]{:S(2)}) collective-permute-start(bf16[768,256]{1,0:T(8,128)(2,1)S(1)} %broadcast_select_fusion.refs_0_), channel_id=1, source_target_pairs={{0,2},{1,3},{2,0},{3,1},{4,6},{5,7},{6,4},{7,5},{8,10},{9,11},{10,... | collective-permute-start | bytes 1179656 | tf_op jit(solution)/shard_map/ppermute | solution.py:18
  22.0 9.4 %collective-permute-start.4 = (bf16[768,256]{1,0:T(8,128)(2,1)S(1)}, bf16[768,256]{1,0:T(8,128)(2,1)S(1)}, u32[]{:S(2)}, u32[]{:S(2)}) collective-permute-start(bf16[768,256]{1,0:T(8,128)(2,1)S(1)} %collective-permute-done.1.refs_0_), channel_id=1, source_target_pairs={{0,2},{1,3},{2,0},{3,1},{4,6},{5,7},{6,4},{7,5},{8,10},{9,11},{10,... | collective-permute-start | bytes 1179656 | tf_op jit(solution)/shard_map/ppermute | solution.py:18
  27.1 4.3 %collective-permute-start.6 = (bf16[768,256]{1,0:T(8,128)(2,1)S(1)}, bf16[768,256]{1,0:T(8,128)(2,1)S(1)}, u32[]{:S(2)}, u32[]{:S(2)}) collective-permute-start(bf16[768,256]{1,0:T(8,128)(2,1)S(1)} %collective-permute-done.5.refs_2_), channel_id=1, source_target_pairs={{0,2},{1,3},{2,0},{3,1},{4,6},{5,7},{6,4},{7,5},{8,10},{9,11},{10,... | collective-permute-start | bytes 1179656 | tf_op jit(solution)/shard_map/ppermute | solution.py:18
  27.1 6.7 %collective-permute-start.3 = (bf16[384,256]{1,0:T(8,128)(2,1)S(1)}, bf16[384,256]{1,0:T(8,128)(2,1)S(1)}, u32[]{:S(2)}, u32[]{:S(2)}) collective-permute-start(bf16[384,256]{1,0:T(8,128)(2,1)S(1)} %get-tuple-element.57), channel_id=1, source_target_pairs={{0,8},{1,9},{2,6},{3,7},{4,12},{5,13},{6,2},{7,3},{8,0},{9,1},{10,... | collective-permute-start | bytes 589832 | tf_op jit(solution)/shard_map/ppermute | solution.py:18
  28.4 5.7 %collective-permute-start.2 = (bf16[384,256]{1,0:T(8,128)(2,1)S(1)}, bf16[384,256]{1,0:T(8,128)(2,1)S(1)}, u32[]{:S(2)}, u32[]{:S(2)}) collective-permute-start(bf16[384,256]{1,0:T(8,128)(2,1)S(1)} %get-tuple-element.58), channel_id=1, source_target_pairs={{0,8},{1,9},{2,6},{3,7},{4,12},{5,13},{6,2},{7,3},{8,0},{9,1},{10,... | collective-permute-start | bytes 589832 | tf_op jit(solution)/shard_map/ppermute | solution.py:18
  34.1 2.8 %collective-permute-start.8 = (bf16[384,256]{1,0:T(8,128)(2,1)S(1)}, bf16[384,256]{1,0:T(8,128)(2,1)S(1)}, u32[]{:S(2)}, u32[]{:S(2)}) collective-permute-start(bf16[384,256]{1,0:T(8,128)(2,1)S(1)} %collective-permute-done.2.refs_0_), channel_id=1, source_target_pairs={{0,2},{1,3},{2,0},{3,1},{4,6},{5,7},{6,4},{7,5},{8,10},{9,11},{10,... | collective-permute-start | bytes 589832 | tf_op jit(solution)/shard_map/ppermute | solution.py:18
  37.6 5.7 %collective-permute-start.11 = (bf16[384,256]{1,0:T(8,128)(2,1)S(1)}, bf16[384,256]{1,0:T(8,128)(2,1)S(1)}, u32[]{:S(2)}, u32[]{:S(2)}) collective-permute-start(bf16[384,256]{1,0:T(8,128)(2,1)S(1)} %get-tuple-element.56), channel_id=1, source_target_pairs={{0,1},{1,0},{2,3},{3,2},{4,5},{5,4},{6,7},{7,6},{8,9},{9,8},{10,11... | collective-permute-start | bytes 589832 | tf_op jit(solution)/shard_map/ppermute | solution.py:18
  37.9 9.6 %collective-permute-start.10 = (bf16[384,256]{1,0:T(8,128)(2,1)S(1)}, bf16[384,256]{1,0:T(8,128)(2,1)S(1)}, u32[]{:S(2)}, u32[]{:S(2)}) collective-permute-start(bf16[384,256]{1,0:T(8,128)(2,1)S(1)} %get-tuple-element.55), channel_id=1, source_target_pairs={{0,1},{1,0},{2,3},{3,2},{4,5},{5,4},{6,7},{7,6},{8,9},{9,8},{10,11... | collective-permute-start | bytes 589832 | tf_op jit(solution)/shard_map/ppermute | solution.py:18
  43.7 9.4 %collective-permute-start.13 = (bf16[384,256]{1,0:T(8,128)(2,1)S(1)}, bf16[384,256]{1,0:T(8,128)(2,1)S(1)}, u32[]{:S(2)}, u32[]{:S(2)}) collective-permute-start(bf16[384,256]{1,0:T(8,128)(2,1)S(1)} %multiply_convert_fusion), channel_id=1, source_target_pairs={{0,16},{3,18},{4,20},{7,22},{8,24},{11,26},{12,28},{15,30},{16,1},... | collective-permute-start | bytes 589832 | tf_op jit(solution)/shard_map/ppermute | solution.py:18
  47.9 13.3 %collective-permute-start.12 = (bf16[384,256]{1,0:T(8,128)(2,1)S(1)}, bf16[384,256]{1,0:T(8,128)(2,1)S(1)}, u32[]{:S(2)}, u32[]{:S(2)}) collective-permute-start(bf16[384,256]{1,0:T(8,128)(2,1)S(1)} %multiply_convert_fusion.1), channel_id=1, source_target_pairs={{0,16},{3,18},{4,20},{7,22},{8,24},{11,26},{12,28},{15,30},{16,1},... | collective-permute-start | bytes 589832 | tf_op jit(solution)/shard_map/ppermute | solution.py:18
  53.2 10.3 %collective-permute-start.15 = (bf16[384,256]{1,0:T(8,128)(2,1)S(1)}, bf16[384,256]{1,0:T(8,128)(2,1)S(1)}, u32[]{:S(2)}, u32[]{:S(2)}) collective-permute-start(bf16[384,256]{1,0:T(8,128)(2,1)S(1)} %broadcast_select_fusion.1.refs_1_), channel_id=1, source_target_pairs={{0,2},{1,3},{2,0},{3,1},{4,6},{5,7},{6,4},{7,5},{8,10},{9,11},{10,... | collective-permute-start | bytes 589832 | tf_op jit(solution)/shard_map/ppermute | solution.py:18
  60.0 4.8 %collective-permute-start.19 = (bf16[384,256]{1,0:T(8,128)(2,1)S(1)}, bf16[384,256]{1,0:T(8,128)(2,1)S(1)}, u32[]{:S(2)}, u32[]{:S(2)}) collective-permute-start(bf16[384,256]{1,0:T(8,128)(2,1)S(1)} %broadcast_select_fusion.1.refs_1_), channel_id=1, source_target_pairs={{0,4},{1,5},{2,10},{3,11},{4,0},{5,1},{6,14},{7,15},{8,12},{9,13},... | collective-permute-start | bytes 589832 | tf_op jit(solution)/shard_map/ppermute | solution.py:18
  60.0 12.3 %collective-permute-start.24 = (bf16[384,256]{1,0:T(8,128)(2,1)S(1)}, bf16[384,256]{1,0:T(8,128)(2,1)S(1)}, u32[]{:S(2)}, u32[]{:S(2)}) collective-permute-start(bf16[384,256]{1,0:T(8,128)(2,1)S(1)} %broadcast_select_fusion.1.refs_1_), channel_id=1, source_target_pairs={{0,8},{1,9},{2,6},{3,7},{4,12},{5,13},{6,2},{7,3},{8,0},{9,1},{10,... | collective-permute-start | bytes 589832 | tf_op jit(solution)/shard_map/ppermute | solution.py:18
  61.3 6.6 %collective-permute-start.14 = (bf16[384,256]{1,0:T(8,128)(2,1)S(1)}, bf16[384,256]{1,0:T(8,128)(2,1)S(1)}, u32[]{:S(2)}, u32[]{:S(2)}) collective-permute-start(bf16[384,256]{1,0:T(8,128)(2,1)S(1)} %broadcast_select_fusion.2.refs_0_), channel_id=1, source_target_pairs={{0,2},{1,3},{2,0},{3,1},{4,6},{5,7},{6,4},{7,5},{8,10},{9,11},{10,... | collective-permute-start | bytes 589832 | tf_op jit(solution)/shard_map/ppermute | solution.py:18
  62.1 10.1 %collective-permute-start.16 = (bf16[384,256]{1,0:T(8,128)(2,1)S(1)}, bf16[384,256]{1,0:T(8,128)(2,1)S(1)}, u32[]{:S(2)}, u32[]{:S(2)}) collective-permute-start(bf16[384,256]{1,0:T(8,128)(2,1)S(1)} %broadcast_select_fusion.2.refs_0_), channel_id=1, source_target_pairs={{0,4},{1,5},{2,10},{3,11},{4,0},{5,1},{6,14},{7,15},{8,12},{9,13},... | collective-permute-start | bytes 589832 | tf_op jit(solution)/shard_map/ppermute | solution.py:18
  63.5 9.2 %collective-permute-start.23 = (bf16[384,256]{1,0:T(8,128)(2,1)S(1)}, bf16[384,256]{1,0:T(8,128)(2,1)S(1)}, u32[]{:S(2)}, u32[]{:S(2)}) collective-permute-start(bf16[384,256]{1,0:T(8,128)(2,1)S(1)} %broadcast_select_fusion.2.refs_0_), channel_id=1, source_target_pairs={{0,8},{1,9},{2,6},{3,7},{4,12},{5,13},{6,2},{7,3},{8,0},{9,1},{10,... | collective-permute-start | bytes 589832 | tf_op jit(solution)/shard_map/ppermute | solution.py:18
  64.8 8.0 %collective-permute-start.22 = (bf16[384,256]{1,0:T(8,128)(2,1)S(1)}, bf16[384,256]{1,0:T(8,128)(2,1)S(1)}, u32[]{:S(2)}, u32[]{:S(2)}) collective-permute-start(bf16[384,256]{1,0:T(8,128)(2,1)S(1)} %collective-permute-done.19.refs_1_), channel_id=1, source_target_pairs={{0,2},{1,3},{2,0},{3,1},{4,6},{5,7},{6,4},{7,5},{8,10},{9,11},{10,... | collective-permute-start | bytes 589832 | tf_op jit(solution)/shard_map/ppermute | solution.py:18
  70.9 7.5 %collective-permute-start.20 = (bf16[384,256]{1,0:T(8,128)(2,1)S(1)}, bf16[384,256]{1,0:T(8,128)(2,1)S(1)}, u32[]{:S(2)}, u32[]{:S(2)}) collective-permute-start(bf16[384,256]{1,0:T(8,128)(2,1)S(1)} %collective-permute-done.19.refs_1_), channel_id=1, source_target_pairs={{0,8},{1,9},{2,6},{3,7},{4,12},{5,13},{6,2},{7,3},{8,0},{9,1},{10,... | collective-permute-start | bytes 589832 | tf_op jit(solution)/shard_map/ppermute | solution.py:18
  72.2 2.0 %collective-permute-start.21 = (bf16[384,256]{1,0:T(8,128)(2,1)S(1)}, bf16[384,256]{1,0:T(8,128)(2,1)S(1)}, u32[]{:S(2)}, u32[]{:S(2)}) collective-permute-start(bf16[384,256]{1,0:T(8,128)(2,1)S(1)} %collective-permute-done.16.refs_0_), channel_id=1, source_target_pairs={{0,2},{1,3},{2,0},{3,1},{4,6},{5,7},{6,4},{7,5},{8,10},{9,11},{10,... | collective-permute-start | bytes 589832 | tf_op jit(solution)/shard_map/ppermute | solution.py:18
  72.2 6.6 %collective-permute-start.17 = (bf16[384,256]{1,0:T(8,128)(2,1)S(1)}, bf16[384,256]{1,0:T(8,128)(2,1)S(1)}, u32[]{:S(2)}, u32[]{:S(2)}) collective-permute-start(bf16[384,256]{1,0:T(8,128)(2,1)S(1)} %collective-permute-done.16.refs_0_), channel_id=1, source_target_pairs={{0,8},{1,9},{2,6},{3,7},{4,12},{5,13},{6,2},{7,3},{8,0},{9,1},{10,... | collective-permute-start | bytes 589832 | tf_op jit(solution)/shard_map/ppermute | solution.py:18
  78.4 2.1 %collective-permute-start.27 = (bf16[384,256]{1,0:T(8,128)(2,1)S(1)}, bf16[384,256]{1,0:T(8,128)(2,1)S(1)}, u32[]{:S(2)}, u32[]{:S(2)}) collective-permute-start(bf16[384,256]{1,0:T(8,128)(2,1)S(1)} %collective-permute-done.20.refs_1_), channel_id=1, source_target_pairs={{0,2},{1,3},{2,0},{3,1},{4,6},{5,7},{6,4},{7,5},{8,10},{9,11},{10,... | collective-permute-start | bytes 589832 | tf_op jit(solution)/shard_map/ppermute | solution.py:18
  (9 other events, 89.6 us)

commit v4 on v3

--- a/solution.py
+++ b/solution.py
@@ -10,7 +10,7 @@
 
 PAIR_ROWS = 128
 EDGE = 8
-UNROLL = 8
+UNROLL = 16
 WIDE = 256
 
 

time: 83.3 us -> 83.2 us (level)
  Pallas kernels: 17.2 us -> 12.7 us
  waiting for transfers between devices: 20.1 us -> 24.1 us
    ppermute x28, waiting for transfers between devices: 20.1 us -> 24.1 us  [permute(): lax.ppermute(block, ('row', 'rep'), [(a[0] * n_rep + a[1], b[0] * n_rep +...]
    pallas_call x4, Pallas kernels: 6.51 us -> 2.5 us  [aggregate(): pl.pallas_call(functools.partial(aggregate_kernel, len(arrays), places, m...]
  transfers between devices with their start and end apart: 28 -> 28, of which waited for: 8 -> 11; matrix products, arithmetic and copies ran while one was open for 3% -> 3% of each run, Pallas kernels for 17% -> 12%
where the time goes in v4:
time: 83.2 us; the launch traced here: 82.4 us
  starting transfers between devices  41.8 us (50%)
  waiting for transfers between devices  24.1 us (29%)
  Pallas kernels  12.7 us (15%)
  matrix products  1.05 us (1%)
  other arithmetic  1.02 us (1%)
  between operations  0.98 us (1%)
    ppermute x28, starting transfers between devices, permute(): lax.ppermute(block, ('row', 'rep'), [(a[0] * n_rep + a[1], b[0] * n_rep +...  41.8 us
    ppermute x28, waiting for transfers between devices, permute(): lax.ppermute(block, ('row', 'rep'), [(a[0] * n_rep + a[1], b[0] * n_rep +...  24.1 us
    pallas_call x4, Pallas kernels, score_pairs(): pl.pallas_call(functools.partial(score_kernel, len(arrays), places, which...  10.2 us
    pallas_call x4, Pallas kernels, aggregate(): pl.pallas_call(functools.partial(aggregate_kernel, len(arrays), places, m...  2.5 us
  transfers between devices with their start and end apart: 28, of which 11 were waited for; matrix products, arithmetic and copies ran while one was open for 3% of the time, Pallas kernels for 12%

profile of v4, /device:TPU:3, one launch (start us, length us, event | category | flops | bytes accessed | tf_op | source)
XLA Modules:
  0.0 82.4 jit_solution(10776086311793429278)
XLA Ops:
  0.7 4.3 %collective-permute-start = (bf16[768,256]{1,0:T(8,128)(2,1)}, bf16[768,256]{1,0:T(8,128)(2,1)S(1)}, u32[]{:S(2)}, u32[]{:S(2)}) collective-permute-start(bf16[768,256]{1,0:T(8,128)(2,1)} %param.8), channel_id=1, source_target_pairs={{0,16},{3,18},{4,20},{7,22},{8,24},{11,26},{12,28},{15,30},{16,1},... | collective-permute-start | bytes 1179656 | tf_op jit(solution)/shard_map/ppermute | solution.py:18
  5.7 9.2 %collective-permute-done = bf16[768,256]{1,0:T(8,128)(2,1)S(1)} collective-permute-done((bf16[768,256]{1,0:T(8,128)(2,1)}, bf16[768,256]{1,0:T(8,128)(2,1)S(1)}, u32[]{:S(2)}, u32[]{:S(2)}) %collective-permute-start) | collective-permute-done | bytes 393248 | tf_op jit(solution)/shard_map/ppermute | solution.py:18
  15.6 1.2 %collective-permute-start.5 = (bf16[768,256]{1,0:T(8,128)(2,1)S(1)}, bf16[768,256]{1,0:T(8,128)(2,1)S(1)}, u32[]{:S(2)}, u32[]{:S(2)}) collective-permute-start(bf16[768,256]{1,0:T(8,128)(2,1)S(1)} %broadcast_select_fusion.refs_0_), channel_id=1, source_target_pairs={{0,8},{1,9},{2,6},{3,7},{4,12},{5,13},{6,2},{7,3},{8,0},{9,1},{10,... | collective-permute-start | bytes 1179656 | tf_op jit(solution)/shard_map/ppermute | solution.py:18
  16.8 2.3 %collective-permute-start.7 = (bf16[768,256]{1,0:T(8,128)(2,1)S(1)}, bf16[768,256]{1,0:T(8,128)(2,1)S(1)}, u32[]{:S(2)}, u32[]{:S(2)}) collective-permute-start(bf16[768,256]{1,0:T(8,128)(2,1)S(1)} %broadcast_select_fusion.refs_0_), channel_id=1, source_target_pairs={{0,2},{1,3},{2,0},{3,1},{4,6},{5,7},{6,4},{7,5},{8,10},{9,11},{10,... | collective-permute-start | bytes 1179656 | tf_op jit(solution)/shard_map/ppermute | solution.py:18
  19.1 2.8 %collective-permute-done.1.refs_0_ = bf16[768,256]{1,0:T(8,128)(2,1)S(1)} collective-permute-done((bf16[768,256]{1,0:T(8,128)(2,1)S(1)}, bf16[768,256]{1,0:T(8,128)(2,1)S(1)}, u32[]{:S(2)}, u32[]{:S(2)}) %collective-permute-start.1) | collective-permute-done | bytes 393248 | tf_op jit(solution)/shard_map/ppermute | solution.py:18
  22.0 5.1 %collective-permute-start.4 = (bf16[768,256]{1,0:T(8,128)(2,1)S(1)}, bf16[768,256]{1,0:T(8,128)(2,1)S(1)}, u32[]{:S(2)}, u32[]{:S(2)}) collective-permute-start(bf16[768,256]{1,0:T(8,128)(2,1)S(1)} %collective-permute-done.1.refs_0_), channel_id=1, source_target_pairs={{0,2},{1,3},{2,0},{3,1},{4,6},{5,7},{6,4},{7,5},{8,10},{9,11},{10,... | collective-permute-start | bytes 1179656 | tf_op jit(solution)/shard_map/ppermute | solution.py:18
  27.1 1.3 %collective-permute-start.3 = (bf16[384,256]{1,0:T(8,128)(2,1)S(1)}, bf16[384,256]{1,0:T(8,128)(2,1)S(1)}, u32[]{:S(2)}, u32[]{:S(2)}) collective-permute-start(bf16[384,256]{1,0:T(8,128)(2,1)S(1)} %get-tuple-element.57), channel_id=1, source_target_pairs={{0,8},{1,9},{2,6},{3,7},{4,12},{5,13},{6,2},{7,3},{8,0},{9,1},{10,... | collective-permute-start | bytes 589832 | tf_op jit(solution)/shard_map/ppermute | solution.py:18
  30.4 1.6 %collective-permute-done.3.refs_1_ = bf16[384,256]{1,0:T(8,128)(2,1)S(1)} collective-permute-done((bf16[384,256]{1,0:T(8,128)(2,1)S(1)}, bf16[384,256]{1,0:T(8,128)(2,1)S(1)}, u32[]{:S(2)}, u32[]{:S(2)}) %collective-permute-start.3) | collective-permute-done | bytes 196640 | tf_op jit(solution)/shard_map/ppermute | solution.py:18
  32.0 2.1 %collective-permute-done.2.refs_0_ = bf16[384,256]{1,0:T(8,128)(2,1)S(1)} collective-permute-done((bf16[384,256]{1,0:T(8,128)(2,1)S(1)}, bf16[384,256]{1,0:T(8,128)(2,1)S(1)}, u32[]{:S(2)}, u32[]{:S(2)}) %collective-permute-start.2) | collective-permute-done | bytes 196640 | tf_op jit(solution)/shard_map/ppermute | solution.py:18
  34.1 1.4 %collective-permute-start.8 = (bf16[384,256]{1,0:T(8,128)(2,1)S(1)}, bf16[384,256]{1,0:T(8,128)(2,1)S(1)}, u32[]{:S(2)}, u32[]{:S(2)}) collective-permute-start(bf16[384,256]{1,0:T(8,128)(2,1)S(1)} %collective-permute-done.2.refs_0_), channel_id=1, source_target_pairs={{0,2},{1,3},{2,0},{3,1},{4,6},{5,7},{6,4},{7,5},{8,10},{9,11},{10,... | collective-permute-start | bytes 589832 | tf_op jit(solution)/shard_map/ppermute | solution.py:18
  37.9 1.5 %collective-permute-start.10 = (bf16[384,256]{1,0:T(8,128)(2,1)S(1)}, bf16[384,256]{1,0:T(8,128)(2,1)S(1)}, u32[]{:S(2)}, u32[]{:S(2)}) collective-permute-start(bf16[384,256]{1,0:T(8,128)(2,1)S(1)} %get-tuple-element.55), channel_id=1, source_target_pairs={{0,1},{1,0},{2,3},{3,2},{4,5},{5,4},{6,7},{7,6},{8,9},{9,8},{10,11... | collective-permute-start | bytes 589832 | tf_op jit(solution)/shard_map/ppermute | solution.py:18
  39.4 4.3 %collective-permute-done.11 = bf16[384,256]{1,0:T(8,128)(2,1)S(1)} collective-permute-done((bf16[384,256]{1,0:T(8,128)(2,1)S(1)}, bf16[384,256]{1,0:T(8,128)(2,1)S(1)}, u32[]{:S(2)}, u32[]{:S(2)}) %collective-permute-start.11) | collective-permute-done | bytes 196640 | tf_op jit(solution)/shard_map/ppermute | solution.py:18
  44.1 4.3 %collective-permute-start.13 = (bf16[384,256]{1,0:T(8,128)(2,1)S(1)}, bf16[384,256]{1,0:T(8,128)(2,1)S(1)}, u32[]{:S(2)}, u32[]{:S(2)}) collective-permute-start(bf16[384,256]{1,0:T(8,128)(2,1)S(1)} %multiply_convert_fusion), channel_id=1, source_target_pairs={{0,16},{3,18},{4,20},{7,22},{8,24},{11,26},{12,28},{15,30},{16,1},... | collective-permute-start | bytes 589832 | tf_op jit(solution)/shard_map/ppermute | solution.py:18
  48.9 3.7 %collective-permute-start.12 = (bf16[384,256]{1,0:T(8,128)(2,1)S(1)}, bf16[384,256]{1,0:T(8,128)(2,1)S(1)}, u32[]{:S(2)}, u32[]{:S(2)}) collective-permute-start(bf16[384,256]{1,0:T(8,128)(2,1)S(1)} %multiply_convert_fusion.1), channel_id=1, source_target_pairs={{0,16},{3,18},{4,20},{7,22},{8,24},{11,26},{12,28},{15,30},{16,1},... | collective-permute-start | bytes 589832 | tf_op jit(solution)/shard_map/ppermute | solution.py:18
  53.8 6.2 %collective-permute-start.15 = (bf16[384,256]{1,0:T(8,128)(2,1)S(1)}, bf16[384,256]{1,0:T(8,128)(2,1)S(1)}, u32[]{:S(2)}, u32[]{:S(2)}) collective-permute-start(bf16[384,256]{1,0:T(8,128)(2,1)S(1)} %broadcast_select_fusion.1.refs_1_), channel_id=1, source_target_pairs={{0,2},{1,3},{2,0},{3,1},{4,6},{5,7},{6,4},{7,5},{8,10},{9,11},{10,... | collective-permute-start | bytes 589832 | tf_op jit(solution)/shard_map/ppermute | solution.py:18
  60.0 1.1 %collective-permute-start.24 = (bf16[384,256]{1,0:T(8,128)(2,1)S(1)}, bf16[384,256]{1,0:T(8,128)(2,1)S(1)}, u32[]{:S(2)}, u32[]{:S(2)}) collective-permute-start(bf16[384,256]{1,0:T(8,128)(2,1)S(1)} %broadcast_select_fusion.1.refs_1_), channel_id=1, source_target_pairs={{0,8},{1,9},{2,6},{3,7},{4,12},{5,13},{6,2},{7,3},{8,0},{9,1},{10,... | collective-permute-start | bytes 589832 | tf_op jit(solution)/shard_map/ppermute | solution.py:18
  62.2 1.3 %collective-permute-start.16 = (bf16[384,256]{1,0:T(8,128)(2,1)S(1)}, bf16[384,256]{1,0:T(8,128)(2,1)S(1)}, u32[]{:S(2)}, u32[]{:S(2)}) collective-permute-start(bf16[384,256]{1,0:T(8,128)(2,1)S(1)} %broadcast_select_fusion.2.refs_0_), channel_id=1, source_target_pairs={{0,4},{1,5},{2,10},{3,11},{4,0},{5,1},{6,14},{7,15},{8,12},{9,13},... | collective-permute-start | bytes 589832 | tf_op jit(solution)/shard_map/ppermute | solution.py:18
  63.8 1.1 %collective-permute-done.19.refs_1_ = bf16[384,256]{1,0:T(8,128)(2,1)S(1)} collective-permute-done((bf16[384,256]{1,0:T(8,128)(2,1)S(1)}, bf16[384,256]{1,0:T(8,128)(2,1)S(1)}, u32[]{:S(2)}, u32[]{:S(2)}) %collective-permute-start.19) | collective-permute-done | bytes 196640 | tf_op jit(solution)/shard_map/ppermute | solution.py:18
  64.9 2.9 %collective-permute-start.22 = (bf16[384,256]{1,0:T(8,128)(2,1)S(1)}, bf16[384,256]{1,0:T(8,128)(2,1)S(1)}, u32[]{:S(2)}, u32[]{:S(2)}) collective-permute-start(bf16[384,256]{1,0:T(8,128)(2,1)S(1)} %collective-permute-done.19.refs_1_), channel_id=1, source_target_pairs={{0,2},{1,3},{2,0},{3,1},{4,6},{5,7},{6,4},{7,5},{8,10},{9,11},{10,... | collective-permute-start | bytes 589832 | tf_op jit(solution)/shard_map/ppermute | solution.py:18
  68.0 2.8 %shard_map.107 = (bf16[384,256]{1,0:T(8,128)(2,1)}, f32[128,128]{1,0:T(8,128)S(1)}, f32[128,128]{1,0:T(8,128)S(1)}) custom-call(s32[256]{0:T(256)S(1)} %select_reduce_fusion.code_ref, s32[5]{0:T(128)S(1)} %convert_reduce_fusion.1.ends_ref, bf16[768,256]{1,0:T(8,128)(2,1)S(1)} %pad_maximum_fusion.emb_ref, ...), custom_call_target="tpu_custom_call" | custom-call | tf_op jit(solution)/shard_map/pallas_call | solution.py:206
  70.8 1.3 %collective-permute-start.20 = (bf16[384,256]{1,0:T(8,128)(2,1)S(1)}, bf16[384,256]{1,0:T(8,128)(2,1)S(1)}, u32[]{:S(2)}, u32[]{:S(2)}) collective-permute-start(bf16[384,256]{1,0:T(8,128)(2,1)S(1)} %collective-permute-done.19.refs_1_), channel_id=1, source_target_pairs={{0,8},{1,9},{2,6},{3,7},{4,12},{5,13},{6,2},{7,3},{8,0},{9,1},{10,... | collective-permute-start | bytes 589832 | tf_op jit(solution)/shard_map/ppermute | solution.py:18
  74.4 3.8 %shard_map.108 = (f32[128,128]{1,0:T(8,128)S(1)}, f32[128,128]{1,0:T(8,128)S(1)}) custom-call(s32[256]{0:T(256)S(1)} %select_reduce_fusion.code_ref, s32[5]{0:T(128)S(1)} %broadcast_maximum_fusion.ends_ref, bf16[768,256]{1,0:T(8,128)(2,1)S(1)} %pad_maximum_fusion.emb_ref, bf16[384,256]{1,0:T(8,128)(2,1)S(1)} %collective-permute-done.16.refs_0_, ...), custom_call_target="tpu_custom_call" | custom-call | tf_op jit(solution)/shard_map/pallas_call | solution.py:206
  78.8 1.5 %shard_map.109 = (f32[128,128]{1,0:T(8,128)S(1)}, f32[128,128]{1,0:T(8,128)S(1)}) custom-call(s32[256]{0:T(256)S(1)} %select_reduce_fusion.code_ref, s32[5]{0:T(128)S(1)} %convert_reduce_fusion.1.ends_ref, bf16[768,256]{1,0:T(8,128)(2,1)S(1)} %pad_maximum_fusion.emb_ref, bf16[384,256]{1,0:T(8,128)(2,1)S(1)} %collective-permute-done.17.refs_0_, ...), custom_call_target="tpu_custom_call" | custom-call | tf_op jit(solution)/shard_map/pallas_call | solution.py:206
  80.3 2.1 %shard_map.110 = (f32[128,128]{1,0:T(8,128)}, f32[128,128]{1,0:T(8,128)}) custom-call(s32[256]{0:T(256)S(1)} %select_reduce_fusion.code_ref, s32[5]{0:T(128)S(1)} %convert_reduce_fusion.1.ends_ref, bf16[768,256]{1,0:T(8,128)(2,1)S(1)} %pad_maximum_fusion.emb_ref, bf16[384,256]{1,0:T(8,128)(2,1)S(1)} %collective-permute-done.18.refs_0_, ...), custom_call_target="tpu_custom_call" | custom-call | tf_op jit(solution)/shard_map/pallas_call | solution.py:206
  (72 shorter events, 12.0 us)
Async XLA Ops:
  0.7 14.3 %collective-permute-start = (bf16[768,256]{1,0:T(8,128)(2,1)}, bf16[768,256]{1,0:T(8,128)(2,1)S(1)}, u32[]{:S(2)}, u32[]{:S(2)}) collective-permute-start(bf16[768,256]{1,0:T(8,128)(2,1)} %param.8), channel_id=1, source_target_pairs={{0,16},{3,18},{4,20},{7,22},{8,24},{11,26},{12,28},{15,30},{16,1},... | collective-permute-start | bytes 1179656 | tf_op jit(solution)/shard_map/ppermute | solution.py:18
  15.0 7.0 %collective-permute-start.1 = (bf16[768,256]{1,0:T(8,128)(2,1)S(1)}, bf16[768,256]{1,0:T(8,128)(2,1)S(1)}, u32[]{:S(2)}, u32[]{:S(2)}) collective-permute-start(bf16[768,256]{1,0:T(8,128)(2,1)S(1)} %broadcast_select_fusion.refs_0_), channel_id=1, source_target_pairs={{0,4},{1,5},{2,10},{3,11},{4,0},{5,1},{6,14},{7,15},{8,12},{9,13},... | collective-permute-start | bytes 1179656 | tf_op jit(solution)/shard_map/ppermute | solution.py:18
  15.6 11.5 %collective-permute-start.5 = (bf16[768,256]{1,0:T(8,128)(2,1)S(1)}, bf16[768,256]{1,0:T(8,128)(2,1)S(1)}, u32[]{:S(2)}, u32[]{:S(2)}) collective-permute-start(bf16[768,256]{1,0:T(8,128)(2,1)S(1)} %broadcast_select_fusion.refs_0_), channel_id=1, source_target_pairs={{0,8},{1,9},{2,6},{3,7},{4,12},{5,13},{6,2},{7,3},{8,0},{9,1},{10,... | collective-permute-start | bytes 1179656 | tf_op jit(solution)/shard_map/ppermute | solution.py:18
  16.8 12.2 %collective-permute-start.7 = (bf16[768,256]{1,0:T(8,128)(2,1)S(1)}, bf16[768,256]{1,0:T(8,128)(2,1)S(1)}, u32[]{:S(2)}, u32[]{:S(2)}) collective-permute-start(bf16[768,256]{1,0:T(8,128)(2,1)S(1)} %broadcast_select_fusion.refs_0_), channel_id=1, source_target_pairs={{0,2},{1,3},{2,0},{3,1},{4,6},{5,7},{6,4},{7,5},{8,10},{9,11},{10,... | collective-permute-start | bytes 1179656 | tf_op jit(solution)/shard_map/ppermute | solution.py:18
  22.0 7.7 %collective-permute-start.4 = (bf16[768,256]{1,0:T(8,128)(2,1)S(1)}, bf16[768,256]{1,0:T(8,128)(2,1)S(1)}, u32[]{:S(2)}, u32[]{:S(2)}) collective-permute-start(bf16[768,256]{1,0:T(8,128)(2,1)S(1)} %collective-permute-done.1.refs_0_), channel_id=1, source_target_pairs={{0,2},{1,3},{2,0},{3,1},{4,6},{5,7},{6,4},{7,5},{8,10},{9,11},{10,... | collective-permute-start | bytes 1179656 | tf_op jit(solution)/shard_map/ppermute | solution.py:18
  27.1 2.6 %collective-permute-start.6 = (bf16[768,256]{1,0:T(8,128)(2,1)S(1)}, bf16[768,256]{1,0:T(8,128)(2,1)S(1)}, u32[]{:S(2)}, u32[]{:S(2)}) collective-permute-start(bf16[768,256]{1,0:T(8,128)(2,1)S(1)} %collective-permute-done.5.refs_2_), channel_id=1, source_target_pairs={{0,2},{1,3},{2,0},{3,1},{4,6},{5,7},{6,4},{7,5},{8,10},{9,11},{10,... | collective-permute-start | bytes 1179656 | tf_op jit(solution)/shard_map/ppermute | solution.py:18
  27.1 4.9 %collective-permute-start.3 = (bf16[384,256]{1,0:T(8,128)(2,1)S(1)}, bf16[384,256]{1,0:T(8,128)(2,1)S(1)}, u32[]{:S(2)}, u32[]{:S(2)}) collective-permute-start(bf16[384,256]{1,0:T(8,128)(2,1)S(1)} %get-tuple-element.57), channel_id=1, source_target_pairs={{0,8},{1,9},{2,6},{3,7},{4,12},{5,13},{6,2},{7,3},{8,0},{9,1},{10,... | collective-permute-start | bytes 589832 | tf_op jit(solution)/shard_map/ppermute | solution.py:18
  28.4 5.7 %collective-permute-start.2 = (bf16[384,256]{1,0:T(8,128)(2,1)S(1)}, bf16[384,256]{1,0:T(8,128)(2,1)S(1)}, u32[]{:S(2)}, u32[]{:S(2)}) collective-permute-start(bf16[384,256]{1,0:T(8,128)(2,1)S(1)} %get-tuple-element.58), channel_id=1, source_target_pairs={{0,8},{1,9},{2,6},{3,7},{4,12},{5,13},{6,2},{7,3},{8,0},{9,1},{10,... | collective-permute-start | bytes 589832 | tf_op jit(solution)/shard_map/ppermute | solution.py:18
  34.1 2.4 %collective-permute-start.8 = (bf16[384,256]{1,0:T(8,128)(2,1)S(1)}, bf16[384,256]{1,0:T(8,128)(2,1)S(1)}, u32[]{:S(2)}, u32[]{:S(2)}) collective-permute-start(bf16[384,256]{1,0:T(8,128)(2,1)S(1)} %collective-permute-done.2.refs_0_), channel_id=1, source_target_pairs={{0,2},{1,3},{2,0},{3,1},{4,6},{5,7},{6,4},{7,5},{8,10},{9,11},{10,... | collective-permute-start | bytes 589832 | tf_op jit(solution)/shard_map/ppermute | solution.py:18
  37.6 6.1 %collective-permute-start.11 = (bf16[384,256]{1,0:T(8,128)(2,1)S(1)}, bf16[384,256]{1,0:T(8,128)(2,1)S(1)}, u32[]{:S(2)}, u32[]{:S(2)}) collective-permute-start(bf16[384,256]{1,0:T(8,128)(2,1)S(1)} %get-tuple-element.56), channel_id=1, source_target_pairs={{0,1},{1,0},{2,3},{3,2},{4,5},{5,4},{6,7},{7,6},{8,9},{9,8},{10,11... | collective-permute-start | bytes 589832 | tf_op jit(solution)/shard_map/ppermute | solution.py:18
  37.9 10.5 %collective-permute-start.10 = (bf16[384,256]{1,0:T(8,128)(2,1)S(1)}, bf16[384,256]{1,0:T(8,128)(2,1)S(1)}, u32[]{:S(2)}, u32[]{:S(2)}) collective-permute-start(bf16[384,256]{1,0:T(8,128)(2,1)S(1)} %get-tuple-element.55), channel_id=1, source_target_pairs={{0,1},{1,0},{2,3},{3,2},{4,5},{5,4},{6,7},{7,6},{8,9},{9,8},{10,11... | collective-permute-start | bytes 589832 | tf_op jit(solution)/shard_map/ppermute | solution.py:18
  44.1 9.5 %collective-permute-start.13 = (bf16[384,256]{1,0:T(8,128)(2,1)S(1)}, bf16[384,256]{1,0:T(8,128)(2,1)S(1)}, u32[]{:S(2)}, u32[]{:S(2)}) collective-permute-start(bf16[384,256]{1,0:T(8,128)(2,1)S(1)} %multiply_convert_fusion), channel_id=1, source_target_pairs={{0,16},{3,18},{4,20},{7,22},{8,24},{11,26},{12,28},{15,30},{16,1},... | collective-permute-start | bytes 589832 | tf_op jit(solution)/shard_map/ppermute | solution.py:18
  48.9 12.3 %collective-permute-start.12 = (bf16[384,256]{1,0:T(8,128)(2,1)S(1)}, bf16[384,256]{1,0:T(8,128)(2,1)S(1)}, u32[]{:S(2)}, u32[]{:S(2)}) collective-permute-start(bf16[384,256]{1,0:T(8,128)(2,1)S(1)} %multiply_convert_fusion.1), channel_id=1, source_target_pairs={{0,16},{3,18},{4,20},{7,22},{8,24},{11,26},{12,28},{15,30},{16,1},... | collective-permute-start | bytes 589832 | tf_op jit(solution)/shard_map/ppermute | solution.py:18
  53.8 9.7 %collective-permute-start.15 = (bf16[384,256]{1,0:T(8,128)(2,1)S(1)}, bf16[384,256]{1,0:T(8,128)(2,1)S(1)}, u32[]{:S(2)}, u32[]{:S(2)}) collective-permute-start(bf16[384,256]{1,0:T(8,128)(2,1)S(1)} %broadcast_select_fusion.1.refs_1_), channel_id=1, source_target_pairs={{0,2},{1,3},{2,0},{3,1},{4,6},{5,7},{6,4},{7,5},{8,10},{9,11},{10,... | collective-permute-start | bytes 589832 | tf_op jit(solution)/shard_map/ppermute | solution.py:18
  60.0 4.9 %collective-permute-start.19 = (bf16[384,256]{1,0:T(8,128)(2,1)S(1)}, bf16[384,256]{1,0:T(8,128)(2,1)S(1)}, u32[]{:S(2)}, u32[]{:S(2)}) collective-permute-start(bf16[384,256]{1,0:T(8,128)(2,1)S(1)} %broadcast_select_fusion.1.refs_1_), channel_id=1, source_target_pairs={{0,4},{1,5},{2,10},{3,11},{4,0},{5,1},{6,14},{7,15},{8,12},{9,13},... | collective-permute-start | bytes 589832 | tf_op jit(solution)/shard_map/ppermute | solution.py:18
  60.0 12.1 %collective-permute-start.24 = (bf16[384,256]{1,0:T(8,128)(2,1)S(1)}, bf16[384,256]{1,0:T(8,128)(2,1)S(1)}, u32[]{:S(2)}, u32[]{:S(2)}) collective-permute-start(bf16[384,256]{1,0:T(8,128)(2,1)S(1)} %broadcast_select_fusion.1.refs_1_), channel_id=1, source_target_pairs={{0,8},{1,9},{2,6},{3,7},{4,12},{5,13},{6,2},{7,3},{8,0},{9,1},{10,... | collective-permute-start | bytes 589832 | tf_op jit(solution)/shard_map/ppermute | solution.py:18
  61.3 6.7 %collective-permute-start.14 = (bf16[384,256]{1,0:T(8,128)(2,1)S(1)}, bf16[384,256]{1,0:T(8,128)(2,1)S(1)}, u32[]{:S(2)}, u32[]{:S(2)}) collective-permute-start(bf16[384,256]{1,0:T(8,128)(2,1)S(1)} %broadcast_select_fusion.2.refs_0_), channel_id=1, source_target_pairs={{0,2},{1,3},{2,0},{3,1},{4,6},{5,7},{6,4},{7,5},{8,10},{9,11},{10,... | collective-permute-start | bytes 589832 | tf_op jit(solution)/shard_map/ppermute | solution.py:18
  62.2 10.0 %collective-permute-start.16 = (bf16[384,256]{1,0:T(8,128)(2,1)S(1)}, bf16[384,256]{1,0:T(8,128)(2,1)S(1)}, u32[]{:S(2)}, u32[]{:S(2)}) collective-permute-start(bf16[384,256]{1,0:T(8,128)(2,1)S(1)} %broadcast_select_fusion.2.refs_0_), channel_id=1, source_target_pairs={{0,4},{1,5},{2,10},{3,11},{4,0},{5,1},{6,14},{7,15},{8,12},{9,13},... | collective-permute-start | bytes 589832 | tf_op jit(solution)/shard_map/ppermute | solution.py:18
  63.5 9.2 %collective-permute-start.23 = (bf16[384,256]{1,0:T(8,128)(2,1)S(1)}, bf16[384,256]{1,0:T(8,128)(2,1)S(1)}, u32[]{:S(2)}, u32[]{:S(2)}) collective-permute-start(bf16[384,256]{1,0:T(8,128)(2,1)S(1)} %broadcast_select_fusion.2.refs_0_), channel_id=1, source_target_pairs={{0,8},{1,9},{2,6},{3,7},{4,12},{5,13},{6,2},{7,3},{8,0},{9,1},{10,... | collective-permute-start | bytes 589832 | tf_op jit(solution)/shard_map/ppermute | solution.py:18
  64.9 8.0 %collective-permute-start.22 = (bf16[384,256]{1,0:T(8,128)(2,1)S(1)}, bf16[384,256]{1,0:T(8,128)(2,1)S(1)}, u32[]{:S(2)}, u32[]{:S(2)}) collective-permute-start(bf16[384,256]{1,0:T(8,128)(2,1)S(1)} %collective-permute-done.19.refs_1_), channel_id=1, source_target_pairs={{0,2},{1,3},{2,0},{3,1},{4,6},{5,7},{6,4},{7,5},{8,10},{9,11},{10,... | collective-permute-start | bytes 589832 | tf_op jit(solution)/shard_map/ppermute | solution.py:18
  70.8 7.4 %collective-permute-start.20 = (bf16[384,256]{1,0:T(8,128)(2,1)S(1)}, bf16[384,256]{1,0:T(8,128)(2,1)S(1)}, u32[]{:S(2)}, u32[]{:S(2)}) collective-permute-start(bf16[384,256]{1,0:T(8,128)(2,1)S(1)} %collective-permute-done.19.refs_1_), channel_id=1, source_target_pairs={{0,8},{1,9},{2,6},{3,7},{4,12},{5,13},{6,2},{7,3},{8,0},{9,1},{10,... | collective-permute-start | bytes 589832 | tf_op jit(solution)/shard_map/ppermute | solution.py:18
  72.1 2.0 %collective-permute-start.21 = (bf16[384,256]{1,0:T(8,128)(2,1)S(1)}, bf16[384,256]{1,0:T(8,128)(2,1)S(1)}, u32[]{:S(2)}, u32[]{:S(2)}) collective-permute-start(bf16[384,256]{1,0:T(8,128)(2,1)S(1)} %collective-permute-done.16.refs_0_), channel_id=1, source_target_pairs={{0,2},{1,3},{2,0},{3,1},{4,6},{5,7},{6,4},{7,5},{8,10},{9,11},{10,... | collective-permute-start | bytes 589832 | tf_op jit(solution)/shard_map/ppermute | solution.py:18
  72.2 6.4 %collective-permute-start.17 = (bf16[384,256]{1,0:T(8,128)(2,1)S(1)}, bf16[384,256]{1,0:T(8,128)(2,1)S(1)}, u32[]{:S(2)}, u32[]{:S(2)}) collective-permute-start(bf16[384,256]{1,0:T(8,128)(2,1)S(1)} %collective-permute-done.16.refs_0_), channel_id=1, source_target_pairs={{0,8},{1,9},{2,6},{3,7},{4,12},{5,13},{6,2},{7,3},{8,0},{9,1},{10,... | collective-permute-start | bytes 589832 | tf_op jit(solution)/shard_map/ppermute | solution.py:18
  78.2 2.1 %collective-permute-start.27 = (bf16[384,256]{1,0:T(8,128)(2,1)S(1)}, bf16[384,256]{1,0:T(8,128)(2,1)S(1)}, u32[]{:S(2)}, u32[]{:S(2)}) collective-permute-start(bf16[384,256]{1,0:T(8,128)(2,1)S(1)} %collective-permute-done.20.refs_1_), channel_id=1, source_target_pairs={{0,2},{1,3},{2,0},{3,1},{4,6},{5,7},{6,4},{7,5},{8,10},{9,11},{10,... | collective-permute-start | bytes 589832 | tf_op jit(solution)/shard_map/ppermute | solution.py:18
  (9 other events, 95.1 us)
